TPU v7x, 256 devices: a whole 4x4x8 slice. The times are simulated.
256 devices in a mesh: row: 4 (over z_hi), col: 64 (over x, z_lo, y, core).
Axes of the slice: x: 4, y: 4, z: 8 (z_hi: 4, z_lo: 2; z = z_hi * 2 + z_lo), core: 2. Of those that a mesh axis runs over, the one named last changes fastest.
Arguments:
- gradient: bfloat16 [2048, 8192], P('row', 'col'), may hold values from -6 to 6
- first_moment: float32 [2048, 8192], P('row', 'col'), may hold values from -2 to 2
- second_moment: float32 [2048, 8192], P('row', 'col'), may hold values from 0.05 to 2
- left_basis: bfloat16 [2048, 2048], P('col', 'row'), may hold values from -0.125 to 0.125
- right_basis: bfloat16 [8192, 8192], P('row', 'col'), may hold values from -0.0625 to 0.0625
Outputs:
- update: float32 [2048, 8192], P('row', 'col')
- first_new: float32 [2048, 8192], P('row', 'col')
- second_new: float32 [2048, 8192], P('row', 'col')
All inputs are finite; a program needn't handle non-finite values.
Results may differ from a plain program's by a relative error of at most 0.004.
Values may be sent and summed in bfloat16 or wider, within the bound.
A program may use at most 64 MiB of HBM per device.

v0:
```python
import jax
import jax.numpy as jnp
from jax import lax
from jax.sharding import PartitionSpec as P

STEP = 10


beta_one = 0.9
beta_two = 0.95
epsilon = 1e-08


def body(gradient, first_moment, second_moment, left_basis, right_basis):
    basis_cols = lax.all_gather(right_basis, "row", axis=0, tiled=True)
    basis_rows = lax.all_to_all(basis_cols, "col", split_axis=0, concat_axis=1, tiled=True)
    left_cols = lax.all_gather(left_basis, "col", axis=0, tiled=True)
    basis_part = basis_cols
    turned_sum = jnp.dot(
        lax.all_gather(gradient, "col", axis=1, tiled=True),
        basis_part,
        preferred_element_type=jnp.float32,
    )
    turned = turned_sum.astype(jnp.bfloat16)
    basis_part = left_cols
    rotated = lax.dot_general(
        basis_part,
        lax.all_gather(turned, "row", axis=0, tiled=True),
        (((0,), (0,)), ((), ())),
        preferred_element_type=jnp.float32,
    )
    first_new = beta_one * first_moment + (1.0 - beta_one) * rotated
    second_new = beta_two * second_moment + (1.0 - beta_two) * rotated * rotated
    corrected_one = first_new / (1.0 - beta_one**STEP)
    corrected_two = second_new / (1.0 - beta_two**STEP)
    scaled = (corrected_one / (jnp.sqrt(corrected_two) + epsilon)).astype(jnp.bfloat16)
    basis_part = left_cols
    back_half = lax.psum_scatter(
        jnp.dot(basis_part, scaled, preferred_element_type=jnp.float32),
        "row",
        scatter_dimension=0,
        tiled=True,
    ).astype(jnp.bfloat16)
    basis_part = basis_rows
    update = lax.dot_general(
        lax.all_gather(back_half, "col", axis=1, tiled=True),
        basis_part,
        (((1,), (1,)), ((), ())),
        preferred_element_type=jnp.float32,
    )
    return (update, first_new, second_new)


def solution(mesh):
    placed = (P("row", "col"), P("row", "col"), P("row", "col"), P("col", "row"), P("row", "col"))
    return jax.shard_map(
        body,
        mesh=mesh,
        in_specs=placed,
        out_specs=(P("row", "col"), P("row", "col"), P("row", "col")),
        check_vma=False,
    )
```

profile of v0, /device:TPU:38, one launch (start us, length us, event | category | flops | bytes accessed | tf_op | source)
XLA Modules:
  0.0 483.9 jit_solution(7032160177536069259)
XLA Ops:
  7.2 0.0 all-gather.7.cloned.1.call-start
  7.2 0.7 all-gather.7.cloned.1.call-update
  7.9 0.0 all-gather.5.cloned.1.call-start
  7.9 0.7 all-gather.5.cloned.1.call-update
  8.6 0.0 all-gather.9.cloned.1.call-start
  8.7 0.7 all-gather.9.cloned.1.call-update
  9.4 0.0 reduce-scatter.2.cloned.1.call-start
  9.4 1.1 copy.16
  10.5 1.1 copy.17
  11.6 52.4 %all-gather.7.cloned.1.call-done = bf16[8192,128]{1,0:T(8,128)(2,1)} async-done(((bf16[2048,128]{1,0:T(8,128)(2,1)}), bf16[8192,128]{1,0:T(8,128)(2,1)}) %all-gather.7.cloned.1.call-update) | async-done | bytes 2097168 | tf_op jit(solution)/shard_map/all_gather | solution.py:15
  64.0 129.1 %all-gather.5.cloned.1.call-done = bf16[512,8192]{1,0:T(8,128)(2,1)} async-done(((bf16[512,128]{1,0:T(8,128)(2,1)}), bf16[512,8192]{1,0:T(8,128)(2,1)}) %all-gather.5.cloned.1.call-update) | async-done | bytes 8388624 | tf_op jit(solution)/shard_map/all_gather | solution.py:20
  193.0 6.3 %convolution_convert_fusion = bf16[512,128]{1,0:T(8,128)(2,1)S(1)} fusion(bf16[512,8192]{1,0:T(8,128)(2,1)} %all-gather.5.cloned.1.call-done, bf16[8192,128]{1,0:T(8,128)(2,1)} %all-gather.7.cloned.1.call-done), kind=kOutput, calls=%fused_computation.2 | convolution fusion | flops 1073807360 | bytes 10616832 | tf_op jit(solution)/shard_map/dot_general | solution.py:19
  199.3 19.4 %all_gather.17 = bf16[2048,128]{1,0:T(8,128)(2,1)S(1)} all-gather(bf16[512,128]{1,0:T(8,128)(2,1)S(1)} %convolution_convert_fusion), channel_id=1, replica_groups=mesh['row'=4,'col'=64] {'row'}, dimensions={0}, use_global_device_ids=true | all-gather | bytes 655360 | tf_op jit(solution)/shard_map/all_gather | solution.py:28
  218.8 81.5 %all-gather.9.cloned.1.call-done = bf16[2048,512]{1,0:T(8,128)(2,1)} async-done(((bf16[32,512]{1,0:T(8,128)(2,1)}), bf16[2048,512]{1,0:T(8,128)(2,1)}) %all-gather.9.cloned.1.call-update) | async-done | bytes 2097168 | tf_op jit(solution)/shard_map/all_gather | solution.py:17
  300.3 0.0 copy-start
  300.3 2.2 multiply_add_fusion
  302.6 0.0 copy-done
  302.6 1.8 convolution_bitcast_fusion
  304.4 0.0 reduce-scatter.2.cloned.1.call-update
  304.4 0.0 all-gather.11.cloned.1.call-start
  304.5 33.8 %reduce-scatter.2.cloned.1.call-done = f32[512,128]{0,1:T(8,128)} async-done(((f32[2048,128]{0,1:T(8,128)}), f32[512,128]{0,1:T(8,128)}) %reduce-scatter.2.cloned.1.call-update) | async-done | bytes 262160 | tf_op jit(solution)/shard_map/reduce_scatter | solution.py:38
  338.3 1.6 convert_element_type.11
  339.9 0.0 all-gather.11.cloned.1.call-update
  339.9 38.5 %all_to_all.19 = bf16[64,128,128]{2,1,0:T(8,128)(2,1)S(1)} all-to-all(bf16[64,128,128]{2,1,0:T(8,128)(2,1)} %bitcast.15), channel_id=1, replica_groups=mesh['row'=4,'col'=64] {'col'}, dimensions={0} | all-to-all | bytes 4194304 | tf_op jit(solution)/shard_map/all_to_all | solution.py:16
  378.5 2.9 copy.18
  381.4 0.8 copy.19
  382.2 0.8 copy.20
  383.1 87.3 %all-gather.11.cloned.1.call-done = bf16[512,8192]{0,1:T(8,128)(2,1)} async-done(((bf16[512,128]{0,1:T(8,128)(2,1)}), bf16[512,8192]{0,1:T(8,128)(2,1)}) %all-gather.11.cloned.1.call-update) | async-done | bytes 8388624 | tf_op jit(solution)/shard_map/all_gather | solution.py:46
  470.3 7.0 %fusion.7 = f32[512,128]{1,0:T(8,128)} fusion(bf16[512,8192]{0,1:T(8,128)(2,1)} %all-gather.11.cloned.1.call-done, bf16[128,8192]{0,1:T(8,128)(2,1)} %bitcast.16), kind=kOutput, calls=%fused_computation.13 | convolution fusion | flops 1073741824 | bytes 10747904 | tf_op jit(solution)/shard_map/dot_general | solution.py:45
Async XLA Ops:
  7.2 56.8 %all-gather.7.cloned.1.call-start = ((), (), s32[]{:S(2)}) async-start(), calls=%async_computation.3 | async-start | bytes 2621440 | tf_op jit(solution)/shard_map/all_gather | solution.py:15
  7.9 185.1 %all-gather.5.cloned.1.call-start = ((), (), s32[]{:S(2)}) async-start(), calls=%async_computation.2 | async-start | bytes 8519680 | tf_op jit(solution)/shard_map/all_gather | solution.py:20
  8.6 291.7 %all-gather.9.cloned.1.call-start = ((), (), s32[]{:S(2)}) async-start(), calls=%async_computation.4 | async-start | bytes 2129920 | tf_op jit(solution)/shard_map/all_gather | solution.py:17
  9.4 328.9 %reduce-scatter.2.cloned.1.call-start = ((), (), s32[]{:S(2)}) async-start(), calls=%async_computation.5 | async-start | bytes 1310720 | tf_op jit(solution)/shard_map/reduce_scatter | solution.py:38
  300.3 2.3 copy-start
  304.4 165.9 %all-gather.11.cloned.1.call-start = ((), (), s32[]{:S(2)}) async-start(), calls=%async_computation.6 | async-start | bytes 8519680 | tf_op jit(solution)/shard_map/all_gather | solution.py:46
Sparse Core Ops, SparseCore 0:
  9.8 54.1 all-gather.6
  65.8 127.2 all-gather.4
  194.9 105.3 all-gather.8
  304.5 33.6 reduce-scatter.1
  340.7 129.5 all-gather.10
where the time goes:
time: 487 us; the launch traced here: 484 us
  waiting for transfers between devices  386 us (79%)
  blocking collectives  58 us (12%)
  matrix products  17.4 us (4%)
  between operations  13.8 us (3%)
  local copies, waits for them, and re-layouts  6.77 us (1%)
    all_gather x1, waiting for transfers between devices, body(): lax.all_gather(gradient, 'col', axis=1, tiled=True)  129 us
    all_gather x1, waiting for transfers between devices, body(): lax.all_gather(back_half, 'col', axis=1, tiled=True)  87.3 us
    all_gather x1, waiting for transfers between devices, body(): left_cols = lax.all_gather(left_basis, 'col', axis=0, tiled=True)  81.5 us
    all_gather x1, waiting for transfers between devices, body(): basis_cols = lax.all_gather(right_basis, 'row', axis=0, tiled=True)  52.4 us
    all_to_all x1, blocking collectives, body(): lax.all_to_all(basis_cols, 'col', split_axis=0, concat_axis=1, tiled=True)  38.5 us
    reduce_scatter x1, waiting for transfers between devices, body(): lax.psum_scatter(jnp.dot(basis_part, scaled, preferred_element_type=jnp.f...  33.8 us
    all_gather x1, blocking collectives, body(): lax.all_gather(turned, 'row', axis=0, tiled=True)  19.4 us
  transfers between devices with their start and end apart: 5, of which 5 were waited for; matrix products, arithmetic and copies ran while one was open for 3% of the time, Pallas kernels for 0%

commit v1 on v0

v1 whole, which is shorter than its diff:
```python
import functools

import jax
import jax.numpy as jnp
from jax import lax
from jax.experimental import pallas as pl
from jax.experimental.pallas import tpu as pltpu
from jax.sharding import PartitionSpec as P

STEP = 10
beta_one = 0.9
beta_two = 0.95
epsilon = 1e-08

MESH = pl.DeviceIdType.MESH
F32 = jnp.float32
BF16 = jnp.bfloat16
SLOTS = 112


def kernel(g, l, r, m, v, upd, fo, so, Gb, Lb, Rb, Rs, Tt, Qb, Bp, Bm, Sb, Ba, Bk, Bs,
           Vb, Rd, W, X, Fb, mb, vb, fb, sb, ssem, rsem, lsem):
    zh = lax.axis_index("row")
    col = lax.axis_index("col")
    c = col % 2
    y = (col // 2) % 4
    zl = (col // 8) % 2
    x = col // 16
    z = 2 * zh + zl

    def dev(x_, y_, z_, c_):
        return (z_ // 2, ((x_ * 2 + z_ % 2) * 4 + y_) * 2 + c_)

    def xn(d):
        return dev((x + d) % 4, y, z, c)

    def yn(d):
        return dev(x, (y + d) % 4, z, c)

    def zn(d):
        return dev(x, y, (z + d) % 8, c)

    sib = dev(x, y, z, 1 - c)
    pair = dev(x, y, 2 * zh + 1 - zl, c)
    g_to = dev(2 * (zh % 2) + 1 - zl, y, 2 * x + zh // 2, c)
    g_from = dev(zh, y, 2 * (2 * zl + x // 2) + 1 - x % 2, c)
    l_xp = 2 * (x % 2) + 1 - zl
    l_to = [dev(l_xp, y, 2 * ((zh + d) % 4) + x // 2, c) for d in range(4)]
    l_from = [dev(2 * zl + x // 2, y, 2 * ((zh + 4 - d) % 4) + 1 - x % 2, c) for d in range(4)]

    slots = {}
    sent = []

    def slot(name):
        return slots.setdefault(name, len(slots))

    def send(name, src, dst, to):
        k = slot(name)
        copy = pltpu.make_async_remote_copy(
            src_ref=src, dst_ref=dst, send_sem=ssem.at[k], recv_sem=rsem.at[k],
            device_id=to, device_id_type=MESH)
        copy.start()
        sent.append(copy)

    def recv(name, dst):
        k = slot(name)
        pltpu.make_async_remote_copy(
            src_ref=dst, dst_ref=dst, send_sem=ssem.at[k], recv_sem=rsem.at[k],
            device_id=sib, device_id_type=MESH).wait_recv()

    own = [
        pltpu.make_async_copy(r, Rb.at[zl], lsem.at[0]),
        pltpu.make_async_copy(m, mb, lsem.at[1]),
        pltpu.make_async_copy(v, vb, lsem.at[2]),
    ]
    for copy in own:
        copy.start()

    barrier = pltpu.get_barrier_semaphore()
    partners = [g_to, g_from, sib, zn(1), zn(7)] + l_to + l_from
    partners += [xn(d) for d in (1, 2, 3)] + [yn(d) for d in (1, 2, 3)]
    for p in partners:
        pl.semaphore_signal(barrier, inc=1, device_id=p, device_id_type=MESH)
    pl.semaphore_wait(barrier, len(partners))

    g_xp = 2 * (zh % 2) + 1 - zl
    for h in range(2):
        send(("gp", h), g.at[h], Gb.at[g_xp, y, c, h], g_to)
    lcols = pl.ds(pl.multiple_of(zh * 512, 512), 512)
    for d in range(4):
        send(("lp", d), l, Lb.at[l_xp, y, c, :, lcols], l_to[d])
    send("rs0", r.at[:, 1 - c], Rs.at[zl], sib)

    recv(("gp", 0), Gb.at[x, y, c, 0])
    for d in (2, 1, 3):
        send(("gx", d), Gb.at[x, y, c, 0], Gb.at[x, y, c, 0], xn(d))
    recv(("gp", 1), Gb.at[x, y, c, 1])
    for d in (2, 1, 3):
        send(("gy", d), Gb.at[x, y, c, 1], Gb.at[x, y, c, 1], yn(d))
    send("rp", r, Rb.at[zl], pair)
    for d in range(4):
        src_zh = (zh + 4 - d) % 4
        recv(("lp", d), Lb.at[x, y, c, :, pl.ds(pl.multiple_of(src_zh * 512, 512), 512)])

    lh = [pl.ds(0, 1024), pl.ds(1024, 1024)]

    for d in (1, 3, 2):
        recv(("gx", d), Gb.at[(x + 4 - d) % 4, y, c, 0])
    lo, hi = pl.ds(0, 2), pl.ds(2, 2)
    send("Gy1a", Gb.at[lo, y, c, 0], Gb.at[lo, y, c, 0], yn(1))
    send("Gy3b", Gb.at[hi, y, c, 0], Gb.at[hi, y, c, 0], yn(3))
    send("Gy1b", Gb.at[hi, y, c, 0], Gb.at[hi, y, c, 0], yn(1))
    send("Gy3a", Gb.at[lo, y, c, 0], Gb.at[lo, y, c, 0], yn(3))
    send("Gs0", Gb.at[:, y, c, 0], Gb.at[:, y, c, 0], sib)
    for d in (1, 3, 2):
        recv(("gy", d), Gb.at[x, (y + 4 - d) % 4, c, 1])
    send("Gx1a", Gb.at[x, lo, c, 1], Gb.at[x, lo, c, 1], xn(1))
    send("Gx3b", Gb.at[x, hi, c, 1], Gb.at[x, hi, c, 1], xn(3))
    send("Gx1b", Gb.at[x, hi, c, 1], Gb.at[x, hi, c, 1], xn(1))
    send("Gx3a", Gb.at[x, lo, c, 1], Gb.at[x, lo, c, 1], xn(3))
    send("Gs1", Gb.at[x, :, c, 1], Gb.at[x, :, c, 1], sib)
    for d in (2, 1, 3):
        send(("lx", d), Lb.at[x, y, c, :, lh[0]], Lb.at[x, y, c, :, lh[0]], xn(d))
        send(("ly", d), Lb.at[x, y, c, :, lh[1]], Lb.at[x, y, c, :, lh[1]], yn(d))

    xm, xp, x2 = (x + 3) % 4, (x + 1) % 4, (x + 2) % 4
    ym, yp, y2 = (y + 3) % 4, (y + 1) % 4, (y + 2) % 4
    recv("Gy1a", Gb.at[lo, ym, c, 0])
    send("Gyfa", Gb.at[lo, ym, c, 0], Gb.at[lo, ym, c, 0], yn(1))
    recv("Gy3b", Gb.at[hi, yp, c, 0])
    send("Gyfb", Gb.at[hi, yp, c, 0], Gb.at[hi, yp, c, 0], yn(3))
    recv("Gx1a", Gb.at[xm, lo, c, 1])
    send("Gxfa", Gb.at[xm, lo, c, 1], Gb.at[xm, lo, c, 1], xn(1))
    recv("Gx3b", Gb.at[xp, hi, c, 1])
    send("Gxfb", Gb.at[xp, hi, c, 1], Gb.at[xp, hi, c, 1], xn(3))
    recv("Gy1b", Gb.at[hi, ym, c, 0])
    send("Gs2", Gb.at[:, ym, c, 0], Gb.at[:, ym, c, 0], sib)
    recv("Gy3a", Gb.at[lo, yp, c, 0])
    send("Gs3", Gb.at[:, yp, c, 0], Gb.at[:, yp, c, 0], sib)
    recv("Gx1b", Gb.at[xm, hi, c, 1])
    send("Gs4", Gb.at[xm, :, c, 1], Gb.at[xm, :, c, 1], sib)
    recv("Gx3a", Gb.at[xp, lo, c, 1])
    send("Gs5", Gb.at[xp, :, c, 1], Gb.at[xp, :, c, 1], sib)

    def lrow(i, h):
        return Lb.at[:, i, c, :, lh[h]]

    def lpart(a, b, h):
        return Lb.at[a, b, c, :, lh[h]]

    for d in (1, 3, 2):
        recv(("lx", d), lpart((x + 4 - d) % 4, y, 0))
    for d in (1, 3, 2):
        recv(("ly", d), lpart(x, (y + 4 - d) % 4, 1))
    for name, a, b, h, to in (
            ("Ly1a", lo, y, 0, yn(1)), ("Ly3b", hi, y, 0, yn(3)),
            ("Lx1a", x, lo, 1, xn(1)), ("Lx3b", x, hi, 1, xn(3)),
            ("Ly1b", hi, y, 0, yn(1)), ("Ly3a", lo, y, 0, yn(3)),
            ("Lx1b", x, hi, 1, xn(1)), ("Lx3a", x, lo, 1, xn(3))):
        send(name, lpart(a, b, h), lpart(a, b, h), to)
    send("Ls0", lpart(slice(None), y, 0), lpart(slice(None), y, 0), sib)
    send("Ls1", lpart(x, slice(None), 1), lpart(x, slice(None), 1), sib)

    recv("Gyfa", Gb.at[lo, y2, c, 0])
    recv("Gyfb", Gb.at[hi, y2, c, 0])
    send("Gs6", Gb.at[:, y2, c, 0], Gb.at[:, y2, c, 0], sib)
    recv("Gxfa", Gb.at[x2, lo, c, 1])
    recv("Gxfb", Gb.at[x2, hi, c, 1])
    send("Gs7", Gb.at[x2, :, c, 1], Gb.at[x2, :, c, 1], sib)
    recv("rp", Rb.at[1 - zl])
    send("rs1", Rb.at[1 - zl, :, 1 - c], Rs.at[1 - zl], sib)

    recv("Ly1a", lpart(lo, ym, 0))
    send("Lyfa", lpart(lo, ym, 0), lpart(lo, ym, 0), yn(1))
    recv("Ly3b", lpart(hi, yp, 0))
    send("Lyfb", lpart(hi, yp, 0), lpart(hi, yp, 0), yn(3))
    recv("Lx1a", lpart(xm, lo, 1))
    send("Lxfa", lpart(xm, lo, 1), lpart(xm, lo, 1), xn(1))
    recv("Lx3b", lpart(xp, hi, 1))
    send("Lxfb", lpart(xp, hi, 1), lpart(xp, hi, 1), xn(3))

    o = 1 - c
    recv("Gs0", Gb.at[:, y, o, 0])
    recv("Gs2", Gb.at[:, ym, o, 0])
    recv("Gs3", Gb.at[:, yp, o, 0])
    recv("Gs6", Gb.at[:, y2, o, 0])
    own[0].wait()

    def turn(b, h):
        lhs = jnp.concatenate(
            [Gb[2 * b + 1 - i, j, k, h] for i in range(2) for j in range(4) for k in range(2)], axis=1)
        rhs = jnp.concatenate([Rb[i].reshape(2048, 128) for i in range(2)], axis=1)
        t = jnp.dot(lhs, rhs, preferred_element_type=F32)
        q = 2 * b + 1 - h
        Tt[:, q * 256:(q + 1) * 256] = t.T.astype(BF16)

    turn(0, 0)
    turn(1, 0)
    recv("Gs1", Gb.at[x, :, o, 1])
    recv("Gs4", Gb.at[xm, :, o, 1])
    recv("Gs5", Gb.at[xp, :, o, 1])
    recv("Gs7", Gb.at[x2, :, o, 1])
    turn(0, 1)
    turn(1, 1)

    recv("Ly1b", lpart(hi, ym, 0))
    send("Ls2", lpart(slice(None), ym, 0), lpart(slice(None), ym, 0), sib)
    recv("Ly3a", lpart(lo, yp, 0))
    send("Ls3", lpart(slice(None), yp, 0), lpart(slice(None), yp, 0), sib)
    recv("Lx1b", lpart(xm, hi, 1))
    send("Ls4", lpart(xm, slice(None), 1), lpart(xm, slice(None), 1), sib)
    recv("Lx3a", lpart(xp, lo, 1))
    send("Ls5", lpart(xp, slice(None), 1), lpart(xp, slice(None), 1), sib)
    recv("Lyfa", lpart(lo, y2, 0))
    recv("Lyfb", lpart(hi, y2, 0))
    send("Ls6", lpart(slice(None), y2, 0), lpart(slice(None), y2, 0), sib)
    recv("Lxfa", lpart(x2, lo, 1))
    recv("Lxfb", lpart(x2, hi, 1))
    send("Ls7", lpart(x2, slice(None), 1), lpart(x2, slice(None), 1), sib)

    def other(a, b, h):
        return Lb.at[a, b, o, :, lh[h]]

    recv("Ls0", other(slice(None), y, 0))
    recv("Ls2", other(slice(None), ym, 0))
    recv("Ls3", other(slice(None), yp, 0))
    recv("Ls6", other(slice(None), y2, 0))
    recv("Ls1", other(x, slice(None), 1))
    recv("Ls4", other(xm, slice(None), 1))
    recv("Ls5", other(xp, slice(None), 1))
    recv("Ls7", other(x2, slice(None), 1))

    def left(k):
        cols = pl.ds(pl.multiple_of(k * 512, 512), 512)
        return Lb[:, :, :, :, cols].reshape(1024, 512)

    def rotate(d):
        k = (zh + d) % 4
        q = jnp.dot(Tt[...], left(k), preferred_element_type=F32)
        Qb[2 * k, 0] = q[0:64].astype(BF16)
        Qb[2 * k, 1] = q[64:128].astype(BF16)
        Qb[2 * k + 1, 0] = q[128:192].astype(BF16)
        Qb[2 * k + 1, 1] = q[192:256].astype(BF16)

    def zi(d):
        return (z + d) % 8

    rotate(2)
    send(("bp", 1, 0), Qb.at[zi(4), 0], Bp.at[0, 0], zn(1))
    send(("bm", 1, 1), Qb.at[zi(4), 1], Bm.at[0, 1], zn(7))
    rotate(1)
    rotate(3)
    send(("bp", 2, 1), Qb.at[zi(3), 1], Bp.at[1, 1], zn(1))
    send(("bm", 2, 0), Qb.at[zi(5), 0], Bm.at[1, 0], zn(7))
    rotate(0)

    def add(k, i, buf, s):
        Qb[k, i] = (Qb[k, i].astype(F32) + buf[s, i].astype(F32)).astype(BF16)

    for s, order in ((2, (0,)), (3, (1, 0)), (4, (1, 0))):
        for i in order:
            j = i
            recv(("bp", s - 1, j), Bp.at[s - 2, j])
            add(zi(5 - s), j, Bp, s - 2)
            send(("bp", s, j), Qb.at[zi(5 - s), j], Bp.at[s - 1, j], zn(1))
            j = 1 - i
            recv(("bm", s - 1, j), Bm.at[s - 2, j])
            add(zi(3 + s), j, Bm, s - 2)
            send(("bm", s, j), Qb.at[zi(3 + s), j], Bm.at[s - 1, j], zn(7))
    own[1].wait()
    own[2].wait()
    for i in range(2):
        recv(("bp", 4, i), Bp.at[3, i])
        recv(("bm", 4, i), Bm.at[3, i])
    total = Qb[z].reshape(128, 512).astype(F32) + Bp[3].reshape(128, 512).astype(F32) \
        + Bm[3].reshape(128, 512).astype(F32)
    rotated = total.T
    first = beta_one * mb[...] + (1.0 - beta_one) * rotated
    second = beta_two * vb[...] + (1.0 - beta_two) * rotated * rotated
    one = first * (1.0 / (1.0 - beta_one**STEP))
    two = second * (1.0 / (1.0 - beta_two**STEP))
    scaled = (one / (jnp.sqrt(two) + epsilon)).astype(BF16)
    Sb[z, 0] = scaled[0:256]
    Sb[z, 1] = scaled[256:512]
    for i in range(2):
        send(("cp", 1, i), Sb.at[z, i], Sb.at[z, i], zn(1))
        send(("cm", 1, i), Sb.at[z, i], Sb.at[z, i], zn(7))
    fb[...] = first
    sb[...] = second
    outs = [pltpu.make_async_copy(fb, fo, lsem.at[3]), pltpu.make_async_copy(sb, so, lsem.at[4])]
    for copy in outs:
        copy.start()

    def back(d, first_part):
        k = (zh + d) % 4
        s = jnp.concatenate([Sb[2 * k].reshape(512, 128), Sb[2 * k + 1].reshape(512, 128)], axis=1)
        part = jnp.dot(left(k), s, preferred_element_type=F32)
        if first_part:
            Ba[...] = part
        else:
            Ba[...] += part

    for s in (2, 3):
        for i in range(2):
            recv(("cp", s - 1, i), Sb.at[zi(9 - s), i])
            send(("cp", s, i), Sb.at[zi(9 - s), i], Sb.at[zi(9 - s), i], zn(1))
            recv(("cm", s - 1, i), Sb.at[zi(s - 1), i])
            send(("cm", s, i), Sb.at[zi(s - 1), i], Sb.at[zi(s - 1), i], zn(7))
        if s == 2:
            back(0, True)
    recv(("cp", 3, 0), Sb.at[zi(5), 0])
    send(("cp", 4, 0), Sb.at[zi(5), 0], Sb.at[zi(5), 0], zn(1))
    recv(("cm", 3, 1), Sb.at[zi(3), 1])
    send(("cm", 4, 1), Sb.at[zi(3), 1], Sb.at[zi(3), 1], zn(7))
    recv(("cp", 3, 1), Sb.at[zi(5), 1])
    recv(("cm", 3, 0), Sb.at[zi(3), 0])
    back(1, False)
    back(3, False)
    recv(("cp", 4, 0), Sb.at[zi(4), 0])
    recv(("cm", 4, 1), Sb.at[zi(4), 1])
    back(2, False)
    Bk[...] = Ba[...].astype(BF16)
    send("bk", Bk, Bs, sib)
    recv("rs0", Rs.at[zl])
    recv("rs1", Rs.at[1 - zl])
    recv("bk", Bs)

    def partial(d):
        k = (x + d) % 4
        rows = pl.ds(pl.multiple_of((k // 2) * 512, 512), 512)
        n = pl.ds((1 - k % 2) * 4, 4)
        lhs = jnp.concatenate([Bk[rows, :], Bs[rows, :]], axis=1)
        rhs = jnp.concatenate(
            [Rb[i, n, c].reshape(512, 128) for i in range(2)] + [Rs[i, n].reshape(512, 128) for i in range(2)],
            axis=1)
        res = lax.dot_general(lhs, rhs, (((1,), (1,)), ((), ())), preferred_element_type=F32).astype(BF16)
        for j in range(4):
            for h in range(2):
                Vb[k, j, h] = res[h * 256:(h + 1) * 256, j * 128:(j + 1) * 128]

    for d in (2, 1, 3):
        partial(d)
        send(("dx", d), Vb.at[(x + d) % 4, :, 1], Rd.at[1, d - 1], xn(d))
    partial(0)
    for d in (2, 1, 3):
        send(("dy", d), Vb.at[:, (y + d) % 4, 0], Rd.at[0, d - 1], yn(d))

    for d in (1, 3, 2):
        recv(("dx", d), Rd.at[1, d - 1])
    W[1] = Vb[x, :, 1].astype(F32) + Rd[1, 0].astype(F32) + Rd[1, 1].astype(F32) + Rd[1, 2].astype(F32)
    for d in (2, 1, 3):
        send(("ey", d), W.at[1, (y + d) % 4], X.at[1, d - 1], yn(d))
    for d in (1, 3, 2):
        recv(("dy", d), Rd.at[0, d - 1])
    W[0] = Vb[:, y, 0].astype(F32) + Rd[0, 0].astype(F32) + Rd[0, 1].astype(F32) + Rd[0, 2].astype(F32)
    for d in (2, 1, 3):
        send(("ex", d), W.at[0, (x + d) % 4], X.at[0, d - 1], xn(d))
    for d in (1, 3, 2):
        recv(("ey", d), X.at[1, d - 1])
    Fb[1] = W[1, y] + X[1, 0] + X[1, 1] + X[1, 2]
    send(("f", 1), Fb.at[1], upd.at[0], g_from)
    for d in (1, 3, 2):
        recv(("ex", d), X.at[0, d - 1])
    Fb[0] = W[0, x] + X[0, 0] + X[0, 1] + X[0, 2]
    send(("f", 0), Fb.at[0], upd.at[1], g_from)
    recv(("f", 1), upd.at[0])
    recv(("f", 0), upd.at[1])
    for copy in outs:
        copy.wait()
    for copy in sent:
        copy.wait_send()
    assert len(slots) <= SLOTS, len(slots)


def body(gradient, first_moment, second_moment, left_basis, right_basis):
    hbm = pl.BlockSpec(memory_space=pl.ANY)
    vm = pltpu.VMEM
    update, first_new, second_new = pl.pallas_call(
        kernel,
        out_shape=(
            jax.ShapeDtypeStruct((2, 256, 128), F32),
            jax.ShapeDtypeStruct((512, 128), F32),
            jax.ShapeDtypeStruct((512, 128), F32),
        ),
        in_specs=[hbm] * 5,
        out_specs=(hbm, hbm, hbm),
        scratch_shapes=[
            vm((4, 4, 2, 2, 256, 128), BF16),
            vm((4, 4, 2, 32, 2048), BF16),
            vm((2, 8, 2, 128, 128), BF16),
            vm((2, 8, 128, 128), BF16),
            vm((256, 1024), BF16),
            vm((8, 2, 64, 512), BF16),
            vm((4, 2, 64, 512), BF16),
            vm((4, 2, 64, 512), BF16),
            vm((8, 2, 256, 128), BF16),
            vm((1024, 256), F32),
            vm((1024, 256), BF16),
            vm((1024, 256), BF16),
            vm((4, 4, 2, 256, 128), BF16),
            vm((2, 3, 4, 256, 128), BF16),
            vm((2, 4, 256, 128), F32),
            vm((2, 3, 256, 128), F32),
            vm((2, 256, 128), F32),
            vm((512, 128), F32),
            vm((512, 128), F32),
            vm((512, 128), F32),
            vm((512, 128), F32),
            pltpu.SemaphoreType.DMA((SLOTS,)),
            pltpu.SemaphoreType.DMA((SLOTS,)),
            pltpu.SemaphoreType.DMA((5,)),
        ],
        compiler_params=pltpu.CompilerParams(
            collective_id=0, has_side_effects=True, vmem_limit_bytes=50 * 2**20),
        cost_estimate=pl.CostEstimate(flops=5 * 10**9, bytes_accessed=10**7, transcendentals=10**5),
    )(
        gradient.reshape(2, 256, 128),
        left_basis,
        right_basis.reshape(8, 2, 128, 128),
        first_moment,
        second_moment,
    )
    return update.reshape(512, 128), first_new, second_new


def solution(mesh):
    place = P("row", "col")
    placed = (place, place, place, P("col", "row"), place)
    return jax.shard_map(
        body, mesh=mesh, in_specs=placed, out_specs=(place, place, place), check_vma=False)
```

time: 487 us -> 131 us (0.27)
  the two profiles are of different devices: /device:TPU:38 before, /device:TPU:136 now
where the time goes in v1:
time: 131 us
  Pallas kernels  123 us (94%)
  local copies, waits for them, and re-layouts  6.7 us (5%)
    pallas_call x1, Pallas kernels, body(): pl.pallas_call(kernel, out_shape=(jax.ShapeDtypeStruct((2, 256, 128), F32...  123 us
    unnamed x13, local copies, waits for them, and re-layouts  6.7 us

profile of v1, /device:TPU:136, one launch (start us, length us, event | category | flops | bytes accessed | tf_op | source)
XLA Modules:
  0.0 130.5 jit_solution(17116858291758874419)
XLA Ops:
  0.6 0.0 copy-start
  0.6 1.0 copy-done
  1.7 0.0 copy-start.1
  1.7 0.9 copy-done.1
  2.6 0.0 copy-start.2
  2.6 0.9 copy-done.2
  3.6 0.0 copy-start.3
  3.6 0.9 copy-done.3
  4.5 0.0 copy-start.4
  4.5 0.8 copy-done.4
  5.2 123.2 %shard_map.76 = (f32[2,256,128]{2,1,0:T(8,128)S(1)}, f32[512,128]{1,0:T(8,128)S(1)}, f32[512,128]{1,0:T(8,128)S(1)}) custom-call(bf16[2,256,128]{2,1,0:T(8,128)(2,1)S(1)} %bitcast.5, bf16[32,512]{1,0:T(8,128)(2,1)S(1)} %copy-done.4, bf16[8,2,128,128]{3,2,1,0:T(8,128)(2,1)S(1)} %bitcast.4, f32[512,128]{1,0:T(8,128)S(1)} %copy-done.1, f32[512,128]{1,0:T(8,128)S(1)} %copy-done.2), custom_call_target="tpu_custom_call" | custom-call | flops 5000000000 | bytes 10000000 | tf_op jit(solution)/shard_map/pallas_call | solution.py:378
  128.4 0.7 copy.11
  129.1 0.7 copy.12
  129.8 0.7 copy.13
Async XLA Ops:
  0.6 1.0 copy-start
  1.7 0.9 copy-start.1
  2.6 0.9 copy-start.2
  3.6 0.9 copy-start.3
  4.5 0.8 copy-start.4

commit v2 on v1

v2 whole, which is shorter than its diff:
```python
import functools

import jax
import jax.numpy as jnp
from jax import lax
from jax.experimental import pallas as pl
from jax.experimental.pallas import tpu as pltpu
from jax.sharding import PartitionSpec as P

STEP = 10
beta_one = 0.9
beta_two = 0.95
epsilon = 1e-08

MESH = pl.DeviceIdType.MESH
F32 = jnp.float32
BF16 = jnp.bfloat16
SLOTS = 176


def kernel(g, l, r, m, v, upd, fo, so, Gx, Gb, Lb, Rb, Rs, Tt, Qb, Bp, Bm, Sb, Ba, Bk, Bs,
           Vb, Rd, W, X, Fb, mb, vb, fb, sb, ssem, rsem, lsem):
    zh = lax.axis_index("row")
    col = lax.axis_index("col")
    c = col % 2
    y = (col // 2) % 4
    zl = (col // 8) % 2
    x = col // 16
    z = 2 * zh + zl

    def dev(x_, y_, z_, c_):
        return (z_ // 2, ((x_ * 2 + z_ % 2) * 4 + y_) * 2 + c_)

    def xn(d):
        return dev((x + d) % 4, y, z, c)

    def yn(d):
        return dev(x, (y + d) % 4, z, c)

    def zn(d):
        return dev(x, y, (z + d) % 8, c)

    def half(k):
        return (1 + (k + 1) // 2) % 2

    sib = dev(x, y, z, 1 - c)
    pair = dev(x, y, 2 * zh + 1 - zl, c)
    b1, b0 = zh // 2, zh % 2
    g_slot = 2 * b0 + zl
    s0 = (x + 4 - zh) % 4
    mine = (zl + half(zh)) % 2
    final_to = dev(zh, y, 2 * (2 * mine + s0 // 2) + s0 % 2, c)
    final_from = dev((g_slot + x) % 4, y, 2 * x + (b1 + half(x)) % 2, c)
    xa = (x + 4 - g_slot) % 4
    z_to = 2 * xa + (b1 + half(xa)) % 2
    z_from = 2 * (2 * mine + s0 // 2) + s0 % 2
    l_slot = 2 * (x % 2) + zl
    t0 = (x + 2 - 2 * half(zh)) % 4
    l_to, l_from = [], []
    for d in range(4):
        k = (zh + d) % 4
        l_to.append(dev((l_slot + 2 - 2 * half(k)) % 4, y, 2 * k + (x // 2 + half(k)) % 2, c))
        k = (zh + 4 - d) % 4
        l_from.append(dev(2 * mine + t0 // 2, y, 2 * k + t0 % 2, c))

    slots = {}
    sent = []

    def slot(name):
        return slots.setdefault(name, len(slots))

    def send(name, src, dst, to):
        k = slot(name)
        copy = pltpu.make_async_remote_copy(
            src_ref=src, dst_ref=dst, send_sem=ssem.at[k], recv_sem=rsem.at[k],
            device_id=to, device_id_type=MESH)
        copy.start()
        sent.append(copy)

    def recv(name, dst):
        k = slot(name)
        pltpu.make_async_remote_copy(
            src_ref=dst, dst_ref=dst, send_sem=ssem.at[k], recv_sem=rsem.at[k],
            device_id=sib, device_id_type=MESH).wait_recv()

    own = [
        pltpu.make_async_copy(r, Rb.at[zl], lsem.at[0]),
        pltpu.make_async_copy(m, mb, lsem.at[1]),
        pltpu.make_async_copy(v, vb, lsem.at[2]),
    ]
    for copy in own:
        copy.start()

    barrier = pltpu.get_barrier_semaphore()
    partners = [final_to, final_from, sib, zn(1), zn(7)] + l_to + l_from
    partners += [dev(x, y, k, jnp.where(k == z, 1 - c, c)) for k in (z_to, z_from)]
    partners += [xn(d) for d in (1, 2, 3)] + [yn(d) for d in (1, 2, 3)]
    for p in partners:
        pl.semaphore_signal(barrier, inc=1, device_id=p, device_id_type=MESH)
    pl.semaphore_wait(barrier, len(partners))

    o = 1 - c
    lo, hi = pl.ds(0, 2), pl.ds(2, 2)
    full = slice(None)
    sm, sp, s2 = (s0 + 3) % 4, (s0 + 1) % 4, (s0 + 2) % 4
    tm, tp, t2 = (t0 + 3) % 4, (t0 + 1) % 4, (t0 + 2) % 4
    ym, yp, y2 = (y + 3) % 4, (y + 1) % 4, (y + 2) % 4

    def same(name, ref, to):
        send(name, ref, ref, to)

    lpos = {2: 0, 3: 512, 1: 1024, 0: 1536}
    for d in (2, 3, 1, 0):
        send(("lp", d), l, Lb.at[l_slot, y, c, :, pl.ds(lpos[d], 512)], l_to[d])
    gm = [slot(("gm", h)) for h in range(2)]

    def move(h):
        return pltpu.make_async_remote_copy(
            src_ref=g.at[h], dst_ref=Gx.at[h], send_sem=ssem.at[gm[h]], recv_sem=rsem.at[gm[h]],
            device_id=dev((x + g_slot) % 4, y, z, c), device_id_type=MESH)

    @pl.when(g_slot != 0)
    def _():
        for h in range(2):
            move(h).start()

    @pl.when(g_slot == 0)
    def _():
        for h in range(2):
            pltpu.make_async_copy(g.at[h], Gx.at[h], rsem.at[gm[h]]).start()

    send("rs0", r.at[:, o], Rs.at[zl], sib)
    gp = [slot(("gp", h)) for h in range(2)]

    def rise(h):
        return pltpu.make_async_remote_copy(
            src_ref=Gx.at[h], dst_ref=Gb.at[g_slot, y, c, h], send_sem=ssem.at[gp[h]], recv_sem=rsem.at[gp[h]],
            device_id=dev(x, y, z_to, c), device_id_type=MESH)

    for h in range(2):
        @pl.when(g_slot != 0)
        def _():
            move(h).wait_recv()

        @pl.when(g_slot == 0)
        def _():
            pltpu.make_async_copy(g.at[h], Gx.at[h], rsem.at[gm[h]]).wait()

        @pl.when(z_to != z)
        def _():
            rise(h).start()

        @pl.when(z_to == z)
        def _():
            pltpu.make_async_copy(Gx.at[h], Gb.at[g_slot, y, c, h], rsem.at[gp[h]]).start()

    def gperm(h):
        @pl.when(z_from != z)
        def _():
            pltpu.make_async_remote_copy(
                src_ref=Gx.at[h], dst_ref=Gb.at[s0, y, c, h], send_sem=ssem.at[gp[h]], recv_sem=rsem.at[gp[h]],
                device_id=sib, device_id_type=MESH).wait_recv()

        @pl.when(z_from == z)
        def _():
            pltpu.make_async_copy(Gx.at[h], Gb.at[s0, y, c, h], rsem.at[gp[h]]).wait()

    def gwait(h):
        if h == 0:
            for d in (1, 3, 2):
                recv(("gx", d), Gb.at[(s0 + 4 - d) % 4, y, c, 0])
        else:
            for d in (1, 3, 2):
                recv(("gy", d), Gb.at[s0, (y + 4 - d) % 4, c, 1])

    lcols = {}
    for j, (at, n) in enumerate(((0, 512), (512, 1024), (1536, 512))):
        lcols[j] = (pl.ds(at, n // 2), pl.ds(at + n // 2, n // 2))

    def lp_(j, h, a, b, core=c):
        return Lb.at[a, b, core, :, lcols[j][h]]

    def lsmall(j):
        for d in (2, 1, 3):
            same(("lx", j, d), lp_(j, 0, t0, y), xn(d))
            same(("ly", j, d), lp_(j, 1, t0, y), yn(d))

    def lbig(j):
        for d in (1, 3, 2):
            recv(("lx", j, d), lp_(j, 0, (t0 + 4 - d) % 4, y))
        same(("Ly1a", j), lp_(j, 0, lo, y), yn(1))
        same(("Ly3b", j), lp_(j, 0, hi, y), yn(3))
        same(("Ly1b", j), lp_(j, 0, hi, y), yn(1))
        same(("Ly3a", j), lp_(j, 0, lo, y), yn(3))
        same(("Ls", j, 0), lp_(j, 0, full, y), sib)
        for d in (1, 3, 2):
            recv(("ly", j, d), lp_(j, 1, t0, (y + 4 - d) % 4))
        same(("Lx1a", j), lp_(j, 1, t0, lo), xn(1))
        same(("Lx3b", j), lp_(j, 1, t0, hi), xn(3))
        same(("Lx1b", j), lp_(j, 1, t0, hi), xn(1))
        same(("Lx3a", j), lp_(j, 1, t0, lo), xn(3))
        same(("Ls", j, 1), lp_(j, 1, t0, full), sib)

    def lfwd(j):
        recv(("Ly1a", j), lp_(j, 0, lo, ym))
        same(("Lyfa", j), lp_(j, 0, lo, ym), yn(1))
        recv(("Ly3b", j), lp_(j, 0, hi, yp))
        same(("Lyfb", j), lp_(j, 0, hi, yp), yn(3))
        recv(("Lx1a", j), lp_(j, 1, tm, lo))
        same(("Lxfa", j), lp_(j, 1, tm, lo), xn(1))
        recv(("Lx3b", j), lp_(j, 1, tp, hi))
        same(("Lxfb", j), lp_(j, 1, tp, hi), xn(3))

    def lshare(j):
        recv(("Ly1b", j), lp_(j, 0, hi, ym))
        same(("Ls", j, 2), lp_(j, 0, full, ym), sib)
        recv(("Ly3a", j), lp_(j, 0, lo, yp))
        same(("Ls", j, 3), lp_(j, 0, full, yp), sib)
        recv(("Lx1b", j), lp_(j, 1, tm, hi))
        same(("Ls", j, 4), lp_(j, 1, tm, full), sib)
        recv(("Lx3a", j), lp_(j, 1, tp, lo))
        same(("Ls", j, 5), lp_(j, 1, tp, full), sib)
        recv(("Lyfa", j), lp_(j, 0, lo, y2))
        recv(("Lyfb", j), lp_(j, 0, hi, y2))
        same(("Ls", j, 6), lp_(j, 0, full, y2), sib)
        recv(("Lxfa", j), lp_(j, 1, t2, lo))
        recv(("Lxfb", j), lp_(j, 1, t2, hi))
        same(("Ls", j, 7), lp_(j, 1, t2, full), sib)

    def lwait(j):
        for i, b in ((0, y), (2, ym), (3, yp), (6, y2)):
            recv(("Ls", j, i), lp_(j, 0, full, b, o))
        for i, a in ((1, t0), (4, tm), (5, tp), (7, t2)):
            recv(("Ls", j, i), lp_(j, 1, a, full, o))

    def lperm(d):
        recv(("lp", d), Lb.at[t0, y, c, :, pl.ds(lpos[d], 512)])

    for d in (2, 3, 1, 0):
        lperm(d)
    for j in range(3):
        lsmall(j)
    @pl.when(z_to != z)
    def _():
        for h in range(2):
            rise(h).wait_send()

    send("rp", r, Rb.at[zl], pair)
    gperm(0)
    for d in (2, 1, 3):
        same(("gx", d), Gb.at[s0, y, c, 0], xn(d))
    gperm(1)
    for d in (2, 1, 3):
        same(("gy", d), Gb.at[s0, y, c, 1], yn(d))
    lbig(0)

    gwait(0)
    same("Gy1a", Gb.at[lo, y, c, 0], yn(1))
    same("Gy3b", Gb.at[hi, y, c, 0], yn(3))
    same("Gy1b", Gb.at[hi, y, c, 0], yn(1))
    same("Gy3a", Gb.at[lo, y, c, 0], yn(3))
    same("Gs0", Gb.at[:, y, c, 0], sib)
    gwait(1)
    same("Gx1a", Gb.at[s0, lo, c, 1], xn(1))
    same("Gx3b", Gb.at[s0, hi, c, 1], xn(3))
    same("Gx1b", Gb.at[s0, hi, c, 1], xn(1))
    same("Gx3a", Gb.at[s0, lo, c, 1], xn(3))
    same("Gs1", Gb.at[s0, :, c, 1], sib)

    lfwd(0)
    recv("Gy1a", Gb.at[lo, ym, c, 0])
    same("Gyfa", Gb.at[lo, ym, c, 0], yn(1))
    recv("Gy3b", Gb.at[hi, yp, c, 0])
    same("Gyfb", Gb.at[hi, yp, c, 0], yn(3))
    recv("Gx1a", Gb.at[sm, lo, c, 1])
    same("Gxfa", Gb.at[sm, lo, c, 1], xn(1))
    recv("Gx3b", Gb.at[sp, hi, c, 1])
    same("Gxfb", Gb.at[sp, hi, c, 1], xn(3))
    lshare(0)
    recv("Gy1b", Gb.at[hi, ym, c, 0])
    same("Gs2", Gb.at[:, ym, c, 0], sib)
    recv("Gy3a", Gb.at[lo, yp, c, 0])
    same("Gs3", Gb.at[:, yp, c, 0], sib)
    recv("Gx1b", Gb.at[sm, hi, c, 1])
    same("Gs4", Gb.at[sm, :, c, 1], sib)
    recv("Gx3a", Gb.at[sp, lo, c, 1])
    same("Gs5", Gb.at[sp, :, c, 1], sib)
    recv("Gyfa", Gb.at[lo, y2, c, 0])
    recv("Gyfb", Gb.at[hi, y2, c, 0])
    same("Gs6", Gb.at[:, y2, c, 0], sib)
    recv("Gxfa", Gb.at[s2, lo, c, 1])
    recv("Gxfb", Gb.at[s2, hi, c, 1])
    same("Gs7", Gb.at[s2, :, c, 1], sib)
    recv("rp", Rb.at[1 - zl])
    send("rs1", Rb.at[1 - zl, :, o], Rs.at[1 - zl], sib)
    lbig(1)

    own[0].wait()
    def turn(b, h):
        lhs = jnp.concatenate(
            [Gb[2 * b + i, j, k, h] for i in range(2) for j in range(4) for k in range(2)], axis=1)
        rhs = jnp.concatenate([Rb[i].reshape(2048, 128) for i in range(2)], axis=1)
        t = jnp.dot(lhs, rhs, preferred_element_type=F32)
        q = 2 * b + h
        Tt[:, q * 256:(q + 1) * 256] = t.T.astype(BF16)

    recv("Gs0", Gb.at[:, y, o, 0])
    recv("Gs2", Gb.at[:, ym, o, 0])
    recv("Gs3", Gb.at[:, yp, o, 0])
    recv("Gs6", Gb.at[:, y2, o, 0])
    turn(0, 0)
    turn(1, 0)
    recv("Gs1", Gb.at[s0, :, o, 1])
    recv("Gs4", Gb.at[sm, :, o, 1])
    recv("Gs5", Gb.at[sp, :, o, 1])
    recv("Gs7", Gb.at[s2, :, o, 1])
    turn(0, 1)
    turn(1, 1)

    lwait(0)

    def left(d):
        at = {2: 0, 1: 512, 3: 1024, 0: 1536}[d]
        return Lb[:, :, :, :, at:at + 512].reshape(1024, 512)

    def rotate(d):
        k = (zh + d) % 4
        q = jnp.dot(Tt[...], left(d), preferred_element_type=F32)
        Qb[2 * k, 0] = q[0:64].astype(BF16)
        Qb[2 * k, 1] = q[64:128].astype(BF16)
        Qb[2 * k + 1, 0] = q[128:192].astype(BF16)
        Qb[2 * k + 1, 1] = q[192:256].astype(BF16)

    def zi(d):
        return (z + d) % 8

    rotate(2)
    send(("bp", 1, 0), Qb.at[zi(4), 0], Bp.at[0, 0], zn(1))
    send(("bm", 1, 1), Qb.at[zi(4), 1], Bm.at[0, 1], zn(7))
    lfwd(1)
    lbig(2)
    lshare(1)
    lwait(1)
    rotate(1)
    rotate(3)
    send(("bp", 2, 1), Qb.at[zi(3), 1], Bp.at[1, 1], zn(1))
    send(("bm", 2, 0), Qb.at[zi(5), 0], Bm.at[1, 0], zn(7))

    def add(k, i, buf, s):
        Qb[k, i] = (Qb[k, i].astype(F32) + buf[s, i].astype(F32)).astype(BF16)

    for s, order in ((2, (0,)), (3, (1, 0)), (4, (1, 0))):
        for i in order:
            j = i
            recv(("bp", s - 1, j), Bp.at[s - 2, j])
            add(zi(5 - s), j, Bp, s - 2)
            send(("bp", s, j), Qb.at[zi(5 - s), j], Bp.at[s - 1, j], zn(1))
            j = 1 - i
            recv(("bm", s - 1, j), Bm.at[s - 2, j])
            add(zi(3 + s), j, Bm, s - 2)
            send(("bm", s, j), Qb.at[zi(3 + s), j], Bm.at[s - 1, j], zn(7))
        if s == 2:
            lfwd(2)
        if s == 3:
            lshare(2)
            lwait(2)
            rotate(0)
    own[1].wait()
    own[2].wait()
    for i in range(2):
        recv(("bp", 4, i), Bp.at[3, i])
        recv(("bm", 4, i), Bm.at[3, i])
    total = Qb[z].reshape(128, 512).astype(F32) + Bp[3].reshape(128, 512).astype(F32) \
        + Bm[3].reshape(128, 512).astype(F32)
    rotated = total.T
    first = beta_one * mb[...] + (1.0 - beta_one) * rotated
    second = beta_two * vb[...] + (1.0 - beta_two) * rotated * rotated
    one = first * (1.0 / (1.0 - beta_one**STEP))
    two = second * (1.0 / (1.0 - beta_two**STEP))
    scaled = (one / (jnp.sqrt(two) + epsilon)).astype(BF16)
    Sb[z, 0] = scaled[0:256]
    Sb[z, 1] = scaled[256:512]
    for i in range(2):
        send(("cp", 1, i), Sb.at[z, i], Sb.at[z, i], zn(1))
        send(("cm", 1, i), Sb.at[z, i], Sb.at[z, i], zn(7))
    fb[...] = first
    sb[...] = second
    outs = [pltpu.make_async_copy(fb, fo, lsem.at[3]), pltpu.make_async_copy(sb, so, lsem.at[4])]
    for copy in outs:
        copy.start()

    def back(d, first_part):
        k = (zh + d) % 4
        s = jnp.concatenate([Sb[2 * k].reshape(512, 128), Sb[2 * k + 1].reshape(512, 128)], axis=1)
        part = jnp.dot(left(d), s, preferred_element_type=F32)
        if first_part:
            Ba[...] = part
        else:
            Ba[...] += part

    for s in (2, 3):
        for i in range(2):
            recv(("cp", s - 1, i), Sb.at[zi(9 - s), i])
            send(("cp", s, i), Sb.at[zi(9 - s), i], Sb.at[zi(9 - s), i], zn(1))
            recv(("cm", s - 1, i), Sb.at[zi(s - 1), i])
            send(("cm", s, i), Sb.at[zi(s - 1), i], Sb.at[zi(s - 1), i], zn(7))
        if s == 2:
            back(0, True)
    recv(("cp", 3, 0), Sb.at[zi(5), 0])
    send(("cp", 4, 0), Sb.at[zi(5), 0], Sb.at[zi(5), 0], zn(1))
    recv(("cm", 3, 1), Sb.at[zi(3), 1])
    send(("cm", 4, 1), Sb.at[zi(3), 1], Sb.at[zi(3), 1], zn(7))
    recv(("cp", 3, 1), Sb.at[zi(5), 1])
    recv(("cm", 3, 0), Sb.at[zi(3), 0])
    back(1, False)
    back(3, False)
    recv(("cp", 4, 0), Sb.at[zi(4), 0])
    recv(("cm", 4, 1), Sb.at[zi(4), 1])
    back(2, False)
    Bk[...] = Ba[...].astype(BF16)
    send("bk", Bk, Bs, sib)
    recv("rs0", Rs.at[zl])
    recv("rs1", Rs.at[1 - zl])
    recv("bk", Bs)

    def partial(k, u):
        rows = [pl.ds(pl.multiple_of((k // 2) * 512 + h * 256 + u * 128, 128), 128) for h in range(2)]
        n = pl.ds((k % 2) * 4, 4)
        lhs = jnp.concatenate(
            [jnp.concatenate([Bk[i, :], Bs[i, :]], axis=1) for i in rows], axis=0)
        rhs = jnp.concatenate(
            [Rb[i, n, c].reshape(512, 128) for i in range(2)] + [Rs[i, n].reshape(512, 128) for i in range(2)],
            axis=1)
        res = lax.dot_general(lhs, rhs, (((1,), (1,)), ((), ())), preferred_element_type=F32).astype(BF16)
        for j in range(4):
            for h in range(2):
                Vb[k, j, h, u] = res[h * 128:(h + 1) * 128, j * 128:(j + 1) * 128]

    for u in range(2):
        for d in (2, 1, 3):
            partial((s0 + d) % 4, u)
            send(("dx", d, u), Vb.at[(s0 + d) % 4, :, 1, u], Rd.at[1, u, d - 1], xn(d))
        partial(s0, u)
        for d in (2, 1, 3):
            send(("dy", d, u), Vb.at[:, (y + d) % 4, 0, u], Rd.at[0, u, d - 1], yn(d))

    def gather_sum(u):
        for d in (1, 3, 2):
            recv(("dx", d, u), Rd.at[1, u, d - 1])
        W[1, u] = Vb[s0, :, 1, u].astype(F32) + Rd[1, u, 0].astype(F32) + Rd[1, u, 1].astype(F32) \
            + Rd[1, u, 2].astype(F32)
        for d in (2, 1, 3):
            send(("ey", d, u), W.at[1, u, (y + d) % 4], X.at[1, u, d - 1], yn(d))
        for d in (1, 3, 2):
            recv(("dy", d, u), Rd.at[0, u, d - 1])
        W[0, u] = Vb[:, y, 0, u].astype(F32) + Rd[0, u, 0].astype(F32) + Rd[0, u, 1].astype(F32) \
            + Rd[0, u, 2].astype(F32)
        for d in (2, 1, 3):
            send(("ex", d, u), W.at[0, u, (s0 + d) % 4], X.at[0, u, d - 1], xn(d))

    def final_sum(u):
        for d in (1, 3, 2):
            recv(("ey", d, u), X.at[1, u, d - 1])
        Fb[1, u] = W[1, u, y] + X[1, u, 0] + X[1, u, 1] + X[1, u, 2]
        send(("f", 1, u), Fb.at[1, u], upd.at[1, u], final_to)
        for d in (1, 3, 2):
            recv(("ex", d, u), X.at[0, u, d - 1])
        Fb[0, u] = W[0, u, s0] + X[0, u, 0] + X[0, u, 1] + X[0, u, 2]
        send(("f", 0, u), Fb.at[0, u], upd.at[0, u], final_to)

    gather_sum(0)
    gather_sum(1)
    final_sum(0)
    final_sum(1)
    for u in range(2):
        recv(("f", 1, u), upd.at[1, u])
        recv(("f", 0, u), upd.at[0, u])
    for copy in outs:
        copy.wait()
    @pl.when(g_slot != 0)
    def _():
        for h in range(2):
            move(h).wait_send()

    for copy in sent:
        copy.wait_send()
    assert len(slots) <= SLOTS, len(slots)


def body(gradient, first_moment, second_moment, left_basis, right_basis):
    hbm = pl.BlockSpec(memory_space=pl.ANY)
    vm = pltpu.VMEM
    update, first_new, second_new = pl.pallas_call(
        kernel,
        out_shape=(
            jax.ShapeDtypeStruct((2, 2, 128, 128), F32),
            jax.ShapeDtypeStruct((512, 128), F32),
            jax.ShapeDtypeStruct((512, 128), F32),
        ),
        in_specs=[hbm] * 5,
        out_specs=(hbm, hbm, hbm),
        scratch_shapes=[
            vm((2, 256, 128), BF16),
            vm((4, 4, 2, 2, 256, 128), BF16),
            vm((4, 4, 2, 32, 2048), BF16),
            vm((2, 8, 2, 128, 128), BF16),
            vm((2, 8, 128, 128), BF16),
            vm((256, 1024), BF16),
            vm((8, 2, 64, 512), BF16),
            vm((4, 2, 64, 512), BF16),
            vm((4, 2, 64, 512), BF16),
            vm((8, 2, 256, 128), BF16),
            vm((1024, 256), F32),
            vm((1024, 256), BF16),
            vm((1024, 256), BF16),
            vm((4, 4, 2, 2, 128, 128), BF16),
            vm((2, 2, 3, 4, 128, 128), BF16),
            vm((2, 2, 4, 128, 128), F32),
            vm((2, 2, 3, 128, 128), F32),
            vm((2, 2, 128, 128), F32),
            vm((512, 128), F32),
            vm((512, 128), F32),
            vm((512, 128), F32),
            vm((512, 128), F32),
            pltpu.SemaphoreType.DMA((SLOTS,)),
            pltpu.SemaphoreType.DMA((SLOTS,)),
            pltpu.SemaphoreType.DMA((5,)),
        ],
        compiler_params=pltpu.CompilerParams(
            collective_id=0, has_side_effects=True, vmem_limit_bytes=63 * 2**20),
        cost_estimate=pl.CostEstimate(flops=5 * 10**9, bytes_accessed=10**7, transcendentals=10**5),
    )(
        gradient.reshape(2, 256, 128),
        left_basis,
        right_basis.reshape(8, 2, 128, 128),
        first_moment,
        second_moment,
    )
    return update.reshape(512, 128), first_new, second_new


def solution(mesh):
    place = P("row", "col")
    placed = (place, place, place, P("col", "row"), place)
    return jax.shard_map(
        body, mesh=mesh, in_specs=placed, out_specs=(place, place, place), check_vma=False)
```

time: 131 us -> 120 us (0.916)
  the two profiles are of different devices: /device:TPU:136 before, /device:TPU:38 now
where the time goes in v2:
time: 120 us; the launch traced here: 118 us
  Pallas kernels  114 us (95%)
  local copies, waits for them, and re-layouts  3.46 us (3%)
    pallas_call x1, Pallas kernels, body(): pl.pallas_call(kernel, out_shape=(jax.ShapeDtypeStruct((2, 2, 128, 128),...  114 us
    unnamed x7, local copies, waits for them, and re-layouts  3.46 us

profile of v2, /device:TPU:38, one launch (start us, length us, event | category | flops | bytes accessed | tf_op | source)
XLA Modules:
  0.0 117.9 jit_solution(865888202058807608)
XLA Ops:
  0.6 113.8 %shard_map.76 = (f32[2,2,128,128]{3,2,1,0:T(8,128)}, f32[512,128]{1,0:T(8,128)}, f32[512,128]{1,0:T(8,128)}) custom-call(bf16[2,256,128]{2,1,0:T(8,128)(2,1)} %bitcast.5, bf16[32,512]{1,0:T(8,128)(2,1)} %l.1, bf16[8,2,128,128]{3,2,1,0:T(8,128)(2,1)} %bitcast.4, f32[512,128]{1,0:T(8,128)} %m.1, f32[512,128]{1,0:T(8,128)} %v.1), custom_call_target="tpu_custom_call" | custom-call | flops 5000000000 | bytes 10000000 | tf_op jit(solution)/shard_map/pallas_call | solution.py:493
  114.4 0.0 copy-start.1
  114.4 1.7 %copy.11 = f32[512,128]{1,0:T(8,128)} copy(f32[512,128]{1,0:T(8,128)} %bitcast.3) | data formatting | bytes 524288
  116.1 0.0 copy-done.1
  116.2 0.0 copy-start
  116.2 0.7 copy.12
  116.9 0.3 copy-done
  117.2 0.7 copy.13
Async XLA Ops:
  114.4 1.7 %copy-start.1 = (f32[512,128]{1,0:T(8,128)S(1)}, f32[512,128]{1,0:T(8,128)}, u32[]{:S(2)}) copy-start(f32[512,128]{1,0:T(8,128)} %get-tuple-element.13) | copy-start | bytes 786436
  116.2 1.0 copy-start

commit v3 on v2

v3 whole, which is shorter than its diff:
```python
import math

import jax
import jax.numpy as jnp
from jax import lax
from jax.experimental import pallas as pl
from jax.experimental.pallas import tpu as pltpu
from jax.sharding import PartitionSpec as P

STEP = 10
beta_one = 0.9
beta_two = 0.95
epsilon = 1e-08

MESH = pl.DeviceIdType.MESH
F32 = jnp.float32
BF16 = jnp.bfloat16
SLOTS = 160


def kernel(g, l, r, m, v, upd, fo, so, Gx, Gb, Lb, Rb, Rs, Tt, Qf, Qs, Bp, Bm, Sb, So, Ba, Bk,
           Vb, Ra, Rd, W, Wb, X, Fb, mb, vb, fb, sb, ssem, rsem, lsem, msem):
    zh = lax.axis_index("row")
    col = lax.axis_index("col")
    c = col % 2
    y = (col // 2) % 4
    zl = (col // 8) % 2
    x = col // 16
    z = 2 * zh + zl

    def dev(x_, y_, z_, c_):
        return (z_ // 2, ((x_ * 2 + z_ % 2) * 4 + y_) * 2 + c_)

    def xn(d):
        return dev((x + d) % 4, y, z, c)

    def yn(d):
        return dev(x, (y + d) % 4, z, c)

    def zn(d):
        return dev(x, y, (z + d) % 8, c)

    def half(k):
        return (1 + (k + 1) // 2) % 2

    sib = dev(x, y, z, 1 - c)
    pair = dev(x, y, 2 * zh + 1 - zl, c)
    b1, b0 = zh // 2, zh % 2
    g_slot = 2 * b0 + zl
    s0 = (x + 4 - zh) % 4
    mine = (zl + half(zh)) % 2
    final_to = dev(zh, y, 2 * (2 * mine + s0 // 2) + s0 % 2, c)
    final_from = dev((g_slot + x) % 4, y, 2 * x + (b1 + half(x)) % 2, c)
    xa = (x + 4 - g_slot) % 4
    z_to = 2 * xa + (b1 + half(xa)) % 2
    z_from = 2 * (2 * mine + s0 // 2) + s0 % 2
    l_slot = 2 * (x % 2) + zl
    t0 = (x + 2 - 2 * half(zh)) % 4
    l_to, l_from = [], []
    for d in range(4):
        k = (zh + d) % 4
        l_to.append(dev((l_slot + 2 - 2 * half(k)) % 4, y, 2 * k + (x // 2 + half(k)) % 2, c))
        k = (zh + 4 - d) % 4
        l_from.append(dev(2 * mine + t0 // 2, y, 2 * k + t0 % 2, c))

    slots = {}
    sent = []

    def slot(name):
        return slots.setdefault(name, len(slots))

    def begin():
        sent.append(0)

    def send(name, src, dst, to):
        k = slot(name)
        pltpu.make_async_remote_copy(
            src_ref=src, dst_ref=dst, send_sem=ssem.at[len(sent) - 1], recv_sem=rsem.at[k],
            device_id=to, device_id_type=MESH).start()
        sent[-1] += math.prod(dst.shape) * dst.dtype.itemsize

    def recv(name, dst):
        pltpu.make_async_remote_copy(
            src_ref=dst, dst_ref=dst, send_sem=ssem.at[0], recv_sem=rsem.at[slot(name)],
            device_id=sib, device_id_type=MESH).wait_recv()

    def left_device(phase):
        rest = sent[phase]
        for unit, ref in ((2**20, Gb), (2**18, Gb.at[0]), (2**17, Gb.at[0, 0]), (2**16, Gb.at[0, 0, 0]),
                          (2**12, Gb.at[0, 0, 0, 0])):
            n, rest = rest // unit, rest % unit
            while n > 0:
                now = min(n, ref.shape[0] if unit > 2**12 else 16)
                part = ref.at[pl.ds(0, now if unit > 2**12 else 16 * now)]
                pltpu.make_async_remote_copy(
                    src_ref=part, dst_ref=part, send_sem=ssem.at[phase], recv_sem=rsem.at[0],
                    device_id=sib, device_id_type=MESH).wait_send()
                n -= now
        assert rest == 0

    begin()
    own = [
        pltpu.make_async_copy(r, Rb.at[zl], lsem.at[0]),
        pltpu.make_async_copy(m, mb, lsem.at[1]),
        pltpu.make_async_copy(v, vb, lsem.at[2]),
    ]
    for copy in own:
        copy.start()

    barrier = pltpu.get_barrier_semaphore()
    partners = [final_to, final_from, sib, zn(1), zn(7)] + l_to + l_from
    partners += [dev(x, y, k, jnp.where(k == z, 1 - c, c)) for k in (z_to, z_from)]
    partners += [xn(d) for d in (1, 2, 3)] + [yn(d) for d in (1, 2, 3)]
    for p in partners:
        pl.semaphore_signal(barrier, inc=1, device_id=p, device_id_type=MESH)
    pl.semaphore_wait(barrier, len(partners))

    o = 1 - c
    lo, hi = pl.ds(0, 2), pl.ds(2, 2)
    full = slice(None)
    sm, sp, s2 = (s0 + 3) % 4, (s0 + 1) % 4, (s0 + 2) % 4
    tm, tp, t2 = (t0 + 3) % 4, (t0 + 1) % 4, (t0 + 2) % 4
    ym, yp, y2 = (y + 3) % 4, (y + 1) % 4, (y + 2) % 4

    def same(name, ref, to):
        send(name, ref, ref, to)

    def lplace(rel, low):
        return {2: 0, 0: 3}.get(rel, 1 + low if rel == 1 else 2 - low)

    for d in (2, 3, 1, 0):
        low = (x // 2 + half((zh + d) % 4)) % 2
        for h in range(2):
            send(("lp", d), l.at[:, pl.ds(h * 256, 256)], Lb.at[l_slot, y, c, lplace((4 - d) % 4, low), h], l_to[d])
    gm = [slot(("gm", h)) for h in range(2)]

    def move(h):
        return pltpu.make_async_remote_copy(
            src_ref=g.at[h], dst_ref=Gx.at[h], send_sem=msem.at[h], recv_sem=rsem.at[gm[h]],
            device_id=dev((x + g_slot) % 4, y, z, c), device_id_type=MESH)

    @pl.when(g_slot != 0)
    def _():
        for h in range(2):
            move(h).start()

    @pl.when(g_slot == 0)
    def _():
        for h in range(2):
            pltpu.make_async_copy(g.at[h], Gx.at[h], rsem.at[gm[h]]).start()

    send("rs0", r.at[:, o], Rs.at[zl], sib)
    gp = [slot(("gp", h)) for h in range(2)]

    def rise(h):
        return pltpu.make_async_remote_copy(
            src_ref=Gx.at[h], dst_ref=Gb.at[g_slot, y, c, h], send_sem=msem.at[2 + h], recv_sem=rsem.at[gp[h]],
            device_id=dev(x, y, z_to, c), device_id_type=MESH)

    for h in range(2):
        @pl.when(g_slot != 0)
        def _():
            move(h).wait_recv()

        @pl.when(g_slot == 0)
        def _():
            pltpu.make_async_copy(g.at[h], Gx.at[h], rsem.at[gm[h]]).wait()

        @pl.when(z_to != z)
        def _():
            rise(h).start()

        @pl.when(z_to == z)
        def _():
            pltpu.make_async_copy(Gx.at[h], Gb.at[g_slot, y, c, h], rsem.at[gp[h]]).start()

    def gperm(h):
        @pl.when(z_from != z)
        def _():
            pltpu.make_async_remote_copy(
                src_ref=Gx.at[h], dst_ref=Gb.at[s0, y, c, h], send_sem=msem.at[2 + h], recv_sem=rsem.at[gp[h]],
                device_id=sib, device_id_type=MESH).wait_recv()

        @pl.when(z_from == z)
        def _():
            pltpu.make_async_copy(Gx.at[h], Gb.at[s0, y, c, h], rsem.at[gp[h]]).wait()

    lcols = (pl.ds(0, 1), pl.ds(1, 2), pl.ds(3, 1))

    def lp_(j, h, a, b):
        return Lb.at[a, b, c, lcols[j], h]

    for d in (2, 3, 1, 0):
        recv(("lp", d), Lb.at[t0, y, c, lplace((4 - d) % 4, zl)])
    for d in (2, 1, 3):
        same("lx", Lb.at[t0, y, c, :, 0], xn(d))
        same("ly", Lb.at[t0, y, c, :, 1], yn(d))

    def lbig(j):
        for d in (1, 3):
            same(("Ly", d, j), lp_(j, 0, full, y), yn(d))
            same(("Lx", d, j), lp_(j, 1, t0, full), xn(d))

    def lfwd(j):
        recv(("Ly", 1, j), lp_(j, 0, full, ym))
        same(("Lyf", j), lp_(j, 0, lo, ym), yn(1))
        recv(("Ly", 3, j), lp_(j, 0, full, yp))
        same(("Lyf", j), lp_(j, 0, hi, yp), yn(3))
        recv(("Lx", 1, j), lp_(j, 1, tm, full))
        same(("Lxf", j), lp_(j, 1, tm, lo), xn(1))
        recv(("Lx", 3, j), lp_(j, 1, tp, full))
        same(("Lxf", j), lp_(j, 1, tp, hi), xn(3))

    def lshare(j):
        recv(("Lyf", j), lp_(j, 0, full, y2))
        recv(("Lxf", j), lp_(j, 1, t2, full))
        for i in {0: (0,), 1: (1, 2), 2: (3,)}[j]:
            same(("Ls", i), Lb.at[:, :, c, i], sib)

    def lwait(i):
        recv(("Ls", i), Lb.at[:, :, o, i])

    @pl.when(z_to != z)
    def _():
        for h in range(2):
            rise(h).wait_send()

    send("rp", r, Rb.at[zl], pair)
    three = pl.ds(0, 3)
    gperm(0)
    for d in (2, 1, 3):
        same("gx", Gb.at[s0, y, c, 0], xn(d))
    gperm(1)
    for d in (2, 1, 3):
        same("gy", Gb.at[s0, y, c, 1], yn(d))
    recv("lx", Lb.at[three, y, c, :, 0])
    recv("ly", Lb.at[t0, three, c, :, 1])
    lbig(0)

    recv("gx", Gb.at[three, y, c, 0])
    same("Gy1a", Gb.at[lo, y, c, 0], yn(1))
    same("Gy3b", Gb.at[hi, y, c, 0], yn(3))
    same("Gy1b", Gb.at[hi, y, c, 0], yn(1))
    same("Gy3a", Gb.at[lo, y, c, 0], yn(3))
    recv("gy", Gb.at[s0, three, c, 1])
    same("Gx1a", Gb.at[s0, lo, c, 1], xn(1))
    same("Gx3b", Gb.at[s0, hi, c, 1], xn(3))
    same("Gx1b", Gb.at[s0, hi, c, 1], xn(1))
    same("Gx3a", Gb.at[s0, lo, c, 1], xn(3))
    same("Gs0", Gb.at[:, y, c, 0], sib)
    same("Gs1", Gb.at[s0, :, c, 1], sib)
    lfwd(0)
    recv("Gy1a", Gb.at[lo, ym, c, 0])
    same("Gyf", Gb.at[lo, ym, c, 0], yn(1))
    recv("Gy3b", Gb.at[hi, yp, c, 0])
    same("Gyf", Gb.at[hi, yp, c, 0], yn(3))
    recv("Gx1a", Gb.at[sm, lo, c, 1])
    same("Gxf", Gb.at[sm, lo, c, 1], xn(1))
    recv("Gx3b", Gb.at[sp, hi, c, 1])
    same("Gxf", Gb.at[sp, hi, c, 1], xn(3))
    lbig(1)
    recv("Gy1b", Gb.at[hi, ym, c, 0])
    same("Gs0", Gb.at[:, ym, c, 0], sib)
    recv("Gy3a", Gb.at[lo, yp, c, 0])
    same("Gs0", Gb.at[:, yp, c, 0], sib)
    recv("Gx1b", Gb.at[sm, hi, c, 1])
    same("Gs1", Gb.at[sm, :, c, 1], sib)
    recv("Gx3a", Gb.at[sp, lo, c, 1])
    same("Gs1", Gb.at[sp, :, c, 1], sib)
    recv("Gyf", Gb.at[:, y2, c, 0])
    same("Gs0", Gb.at[:, y2, c, 0], sib)
    recv("Gxf", Gb.at[s2, :, c, 1])
    same("Gs1", Gb.at[s2, :, c, 1], sib)
    lshare(0)
    recv("rp", Rb.at[1 - zl])
    send("rs1", Rb.at[1 - zl, :, o], Rs.at[1 - zl], sib)

    own[0].wait()
    def turn(b, h):
        lhs = jnp.concatenate(
            [Gb[2 * b + i, j, k, h] for i in range(2) for j in range(4) for k in range(2)], axis=1)
        rhs = jnp.concatenate([Rb[i].reshape(2048, 128) for i in range(2)], axis=1)
        t = jnp.dot(lhs, rhs, preferred_element_type=F32)
        q = 2 * b + h
        Tt[:, q * 256:(q + 1) * 256] = t.T.astype(BF16)

    recv("Gs0", Gb.at[:, :, o, 0])
    turn(0, 0)
    turn(1, 0)
    lfwd(1)
    recv("Gs1", Gb.at[:, :, o, 1])
    turn(0, 1)
    turn(1, 1)

    lwait(0)

    def left(j):
        return jnp.concatenate([Lb[:, :, :, j, h].reshape(1024, 256) for h in range(2)], axis=1)

    rels = (2, 1 + 2 * zl, 3 - 2 * zl, 0)

    def rotate(p):
        k = (zh + rels[p]) % 4
        q = jnp.dot(Tt[...], left(p), preferred_element_type=F32)
        for i in range(2):
            for j in range(2):
                part = q[i * 128:(i + 1) * 128, j * 256:(j + 1) * 256]
                Qf[2 * k + i, j] = part
                Qs[2 * k + i, j] = part.astype(BF16)

    def zi(d):
        return (z + d) % 8

    ha, hb = pl.ds(0, 64), pl.ds(64, 64)
    rotate(0)
    for j in range(2):
        send(("bp", 1, j), Qs.at[zi(4), j, ha], Bp.at[0, j, ha], zn(1))
        send(("bm", 1, j), Qs.at[zi(4), j, hb], Bm.at[0, j, hb], zn(7))
    lshare(1)
    lbig(2)
    lwait(1)
    rotate(1)
    send("bpe", Qs.at[zi(3), :, hb], Bp.at[1, :, hb], zn(1))
    send("bme", Qs.at[zi(5), :, ha], Bm.at[1, :, ha], zn(7))

    for j in range(2):
        k = zi(3)
        recv(("bp", 1, j), Bp.at[0, j, ha])
        Qs[k, j, ha] = (Qf[k, j, ha] + Bp[0, j, ha].astype(F32)).astype(BF16)
        send(("bp", 2, j), Qs.at[k, j, ha], Bp.at[1, j, ha], zn(1))
        k = zi(5)
        recv(("bm", 1, j), Bm.at[0, j, hb])
        Qs[k, j, hb] = (Qf[k, j, hb] + Bm[0, j, hb].astype(F32)).astype(BF16)
        send(("bm", 2, j), Qs.at[k, j, hb], Bm.at[1, j, hb], zn(7))
    lwait(2)
    rotate(2)
    lfwd(2)
    recv("bpe", Bp.at[1, :, hb])
    recv("bme", Bm.at[1, :, ha])
    for s in (3, 4):
        for j in range(2):
            k = zi(5 - s)
            recv(("bp", s - 1, j), Bp.at[s - 2, j] if s > 3 else Bp.at[1, j, ha])
            Qs[k, j] = (Qf[k, j] + Bp[s - 2, j].astype(F32)).astype(BF16)
            send(("bp", s, j), Qs.at[k, j], Bp.at[s - 1, j], zn(1))
            k = zi(3 + s)
            recv(("bm", s - 1, j), Bm.at[s - 2, j] if s > 3 else Bm.at[1, j, hb])
            Qs[k, j] = (Qf[k, j] + Bm[s - 2, j].astype(F32)).astype(BF16)
            send(("bm", s, j), Qs.at[k, j], Bm.at[s - 1, j], zn(7))
        if s == 3:
            lshare(2)
            lwait(3)
            rotate(3)
    own[1].wait()
    own[2].wait()
    begin()
    for j in range(2):
        recv(("bp", 4, j), Bp.at[3, j])
        recv(("bm", 4, j), Bm.at[3, j])
        rows = slice(j * 256, (j + 1) * 256)
        rotated = (Qf[z, j] + Bp[3, j].astype(F32) + Bm[3, j].astype(F32)).T
        first = beta_one * mb[rows] + (1.0 - beta_one) * rotated
        second = beta_two * vb[rows] + (1.0 - beta_two) * rotated * rotated
        one = first * (1.0 / (1.0 - beta_one**STEP))
        two = second * (1.0 / (1.0 - beta_two**STEP))
        scaled = (one / (jnp.sqrt(two) + epsilon)).astype(BF16)
        for i in (2 * j, 2 * j + 1):
            Sb[z, i] = scaled[(i - 2 * j) * 128:(i - 2 * j + 1) * 128]
            same(("cp", 1, i), Sb.at[z, i], zn(1))
            same(("cm", 1, i), Sb.at[z, i], zn(7))
        fb[rows] = first
        sb[rows] = second
    outs = [pltpu.make_async_copy(fb, fo, lsem.at[3]), pltpu.make_async_copy(sb, so, lsem.at[4])]
    for copy in outs:
        copy.start()

    left_device(0)
    def across(d):
        send(("ss", d), Sb.at[zi(d)], So.at[zi(d)], sib)

    def crossed(*ds):
        for d in ds:
            recv(("ss", d), So.at[zi(d)])

    def back(j, first_part):
        k = (zh + rels[j]) % 4
        s = jnp.concatenate(
            [ref[2 * k + i].reshape(512, 128) for ref in (Sb, So) for i in range(2)], axis=1)
        part = jnp.dot(left(j), s, preferred_element_type=F32)
        if first_part:
            Ba[...] = part
        else:
            Ba[...] += part

    across(0)
    for s in (2, 3):
        for j in range(4):
            recv(("cp", s - 1, j), Sb.at[zi(9 - s), j])
            same(("cp", s, j), Sb.at[zi(9 - s), j], zn(1))
            recv(("cm", s - 1, j), Sb.at[zi(s - 1), j])
            same(("cm", s, j), Sb.at[zi(s - 1), j], zn(7))
        across(9 - s)
        across(s - 1)
    crossed(0, 1, 7)
    back(3, True)
    for j in range(2):
        recv(("cp", 3, j), Sb.at[zi(5), j])
        same(("cp", 4, j), Sb.at[zi(5), j], zn(1))
        recv(("cm", 3, j + 2), Sb.at[zi(3), j + 2])
        same(("cm", 4, j + 2), Sb.at[zi(3), j + 2], zn(7))
    for j in range(2):
        recv(("cp", 3, j + 2), Sb.at[zi(5), j + 2])
        recv(("cm", 3, j), Sb.at[zi(3), j])
    across(5)
    across(3)
    crossed(2, 6, 3, 5)
    back(1, False)
    back(2, False)
    for j in range(2):
        recv(("cp", 4, j), Sb.at[zi(4), j])
        recv(("cm", 4, j + 2), Sb.at[zi(4), j + 2])
    across(4)
    crossed(4)
    back(0, False)
    Bk[...] = Ba[...].astype(BF16)
    recv("rs0", Rs.at[zl])
    recv("rs1", Rs.at[1 - zl])
    def partial(k, pair_of_parts, is_own):
        rows = [pl.ds(pl.multiple_of((k // 2) * 512 + h * 256 + pair_of_parts * 128, 128), 128) for h in range(2)]
        n = pl.ds((k % 2) * 4, 4)
        lhs = jnp.concatenate([Bk[i, :] for i in rows], axis=0)
        rhs = jnp.concatenate(
            [Rb[i, n, c].reshape(512, 128) for i in range(2)] + [Rs[i, n].reshape(512, 128) for i in range(2)],
            axis=1)
        res = lax.dot_general(lhs, rhs, (((1,), (1,)), ((), ())), preferred_element_type=F32)
        for i in range(2):
            u = 2 * pair_of_parts + i
            top, low = res[i * 64:i * 64 + 64], res[128 + i * 64:192 + i * 64]
            kept = top[:, 0:128]
            for j in range(4):
                at = slice(j * 128, (j + 1) * 128)
                Vb[k, j, 0, u] = top[:, at].astype(BF16)
                if j > 0:
                    kept = jnp.where(y == j, top[:, at], kept)
                if is_own:
                    W[1, u, j] = low[:, at]
                else:
                    Vb[k, j, 1, u] = low[:, at].astype(BF16)
            W[0, u, k] = kept

    def send_far(u):
        send(("dx", 1, u), Vb.at[s2, lo, 1, u], Ra.at[1, u, 0], xn(1))
        send(("dx", 3, u), Vb.at[s2, hi, 1, u], Ra.at[1, u, 1], xn(3))
        send(("dy", 1, u), Vb.at[lo, y2, 0, u], Ra.at[0, u, 0], yn(1))
        send(("dy", 3, u), Vb.at[hi, y2, 0, u], Ra.at[0, u, 1], yn(3))

    def send_near(u):
        for i, part, a, b, d in ((0, lo, sp, yp, 1), (1, hi, sm, ym, 3)):
            recv(("dx", d, u), Ra.at[1, u, i])
            Vb[a, part, 1, u] = (Vb[a, part, 1, u].astype(F32) + Ra[1, u, i].astype(F32)).astype(BF16)
            send(("nx", u), Vb.at[a, :, 1, u], Rd.at[1, u, i], xn(d))
            recv(("dy", d, u), Ra.at[0, u, i])
            Vb[part, b, 0, u] = (Vb[part, b, 0, u].astype(F32) + Ra[0, u, i].astype(F32)).astype(BF16)
            send(("ny", u), Vb.at[:, b, 0, u], Rd.at[0, u, i], yn(d))

    def send_small(u):
        for h, name, small, step in ((1, "nx", "ey", yn), (0, "ny", "ex", xn)):
            recv((name, u), Rd.at[h, u])
            total = W[h, u] + Rd[h, u, 0].astype(F32) + Rd[h, u, 1].astype(F32)
            W[h, u] = total
            Wb[h, u] = total.astype(BF16)
            for d in (2, 1, 3):
                at = (y + d) % 4 if h == 1 else (s0 + d) % 4
                send((small, u), Wb.at[h, u, at], X.at[h, u, d - 1], step(d))

    def send_final(u):
        for h, small, at in ((1, "ey", y), (0, "ex", s0)):
            recv((small, u), X.at[h, u])
            Fb[h, u] = W[h, u, at] + X[h, u, 0].astype(F32) + X[h, u, 1].astype(F32) + X[h, u, 2].astype(F32)
            send("f", Fb.at[h, u], upd.at[pl.ds(h * 256 + u * 64, 64)], final_to)

    begin()
    for i in range(2):
        for k in (s2, sp, sm):
            partial(k, i, False)
        partial(s0, i, True)
        send_far(2 * i)
        send_far(2 * i + 1)
    send_near(0)
    send_near(1)
    left_device(1)
    send_small(0)
    send_near(2)
    send_small(1)
    send_near(3)
    send_final(0)
    send_small(2)
    send_final(1)
    send_small(3)
    send_final(2)
    send_final(3)
    @pl.when(g_slot != 0)
    def _():
        for h in range(2):
            move(h).wait_send()

    left_device(2)
    recv("f", upd)
    for copy in outs:
        copy.wait()
    assert len(slots) <= SLOTS, len(slots)


def body(gradient, first_moment, second_moment, left_basis, right_basis):
    hbm = pl.BlockSpec(memory_space=pl.ANY)
    vm = pltpu.VMEM
    update, first_new, second_new = pl.pallas_call(
        kernel,
        out_shape=(
            jax.ShapeDtypeStruct((512, 128), F32),
            jax.ShapeDtypeStruct((512, 128), F32),
            jax.ShapeDtypeStruct((512, 128), F32),
        ),
        in_specs=[hbm] * 5,
        out_specs=(hbm, hbm, hbm),
        scratch_shapes=[
            vm((2, 256, 128), BF16),
            vm((4, 4, 2, 2, 256, 128), BF16),
            vm((4, 4, 2, 4, 2, 32, 256), BF16),
            vm((2, 8, 2, 128, 128), BF16),
            vm((2, 8, 128, 128), BF16),
            vm((256, 1024), BF16),
            vm((8, 2, 128, 256), F32),
            vm((8, 2, 128, 256), BF16),
            vm((4, 2, 128, 256), BF16),
            vm((4, 2, 128, 256), BF16),
            vm((8, 4, 128, 128), BF16),
            vm((8, 4, 128, 128), BF16),
            vm((1024, 512), F32),
            vm((1024, 512), BF16),
            vm((4, 4, 2, 4, 64, 128), BF16),
            vm((2, 4, 2, 2, 64, 128), BF16),
            vm((2, 4, 2, 4, 64, 128), BF16),
            vm((2, 4, 4, 64, 128), F32),
            vm((2, 4, 4, 64, 128), BF16),
            vm((2, 4, 3, 64, 128), BF16),
            vm((2, 4, 64, 128), F32),
            vm((512, 128), F32),
            vm((512, 128), F32),
            vm((512, 128), F32),
            vm((512, 128), F32),
            pltpu.SemaphoreType.DMA((8,)),
            pltpu.SemaphoreType.DMA((SLOTS,)),
            pltpu.SemaphoreType.DMA((5,)),
            pltpu.SemaphoreType.DMA((4,)),
        ],
        compiler_params=pltpu.CompilerParams(
            collective_id=0, has_side_effects=True, vmem_limit_bytes=63 * 2**20),
        cost_estimate=pl.CostEstimate(flops=5 * 10**9, bytes_accessed=10**7, transcendentals=10**5),
    )(
        gradient.reshape(2, 256, 128),
        left_basis,
        right_basis.reshape(8, 2, 128, 128),
        first_moment,
        second_moment,
    )
    return update, first_new, second_new


def solution(mesh):
    place = P("row", "col")
    placed = (place, place, place, P("col", "row"), place)
    return jax.shard_map(
        body, mesh=mesh, in_specs=placed, out_specs=(place, place, place), check_vma=False)
```

time: 120 us -> 108 us (0.900); the launches traced: 118 us -> 107 us
  Pallas kernels: 114 us -> 103 us
    pallas_call x1, Pallas kernels: 114 us -> 103 us  [body(): pl.pallas_call(kernel, out_shape=(jax.ShapeDtypeStruct((512, 128), F32),...]
where the time goes in v3:
time: 108 us; the launch traced here: 107 us
  Pallas kernels  103 us (95%)
  local copies, waits for them, and re-layouts  3.46 us (3%)
    pallas_call x1, Pallas kernels, body(): pl.pallas_call(kernel, out_shape=(jax.ShapeDtypeStruct((512, 128), F32),...  103 us
    unnamed x7, local copies, waits for them, and re-layouts  3.46 us

profile of v3, /device:TPU:38, one launch (start us, length us, event | category | flops | bytes accessed | tf_op | source)
XLA Modules:
  0.0 107.3 jit_solution(10241465554968709729)
XLA Ops:
  0.6 103.2 %shard_map.76 = (f32[512,128]{1,0:T(8,128)}, f32[512,128]{1,0:T(8,128)}, f32[512,128]{1,0:T(8,128)}) custom-call(bf16[2,256,128]{2,1,0:T(8,128)(2,1)} %bitcast.3, bf16[32,512]{1,0:T(8,128)(2,1)} %l.1, bf16[8,2,128,128]{3,2,1,0:T(8,128)(2,1)} %bitcast.2, f32[512,128]{1,0:T(8,128)} %m.1, f32[512,128]{1,0:T(8,128)} %v.1), custom_call_target="tpu_custom_call" | custom-call | flops 5000000000 | bytes 10000000 | tf_op jit(solution)/shard_map/pallas_call | solution.py:517
  103.8 0.0 copy-start.1
  103.8 1.7 %copy.11 = f32[512,128]{1,0:T(8,128)} copy(f32[512,128]{1,0:T(8,128)} %get-tuple-element.6) | data formatting | bytes 524288
  105.5 0.0 copy-done.1
  105.5 0.0 copy-start
  105.5 0.7 copy.12
  106.2 0.3 copy-done
  106.6 0.7 copy.13
Async XLA Ops:
  103.8 1.7 %copy-start.1 = (f32[512,128]{1,0:T(8,128)S(1)}, f32[512,128]{1,0:T(8,128)}, u32[]{:S(2)}) copy-start(f32[512,128]{1,0:T(8,128)} %get-tuple-element.7) | copy-start | bytes 786436
  105.5 1.0 copy-start

commit v4 on v3

--- a/solution.py
+++ b/solution.py
@@ -303,8 +303,8 @@
         k = (zh + rels[p]) % 4
         q = jnp.dot(Tt[...], left(p), preferred_element_type=F32)
         for i in range(2):
-            for j in range(2):
-                part = q[i * 128:(i + 1) * 128, j * 256:(j + 1) * 256]
+            for j in range(4):
+                part = q[i * 128:(i + 1) * 128, j * 128:(j + 1) * 128]
                 Qf[2 * k + i, j] = part
                 Qs[2 * k + i, j] = part.astype(BF16)
 
@@ -313,7 +313,7 @@
 
     ha, hb = pl.ds(0, 64), pl.ds(64, 64)
     rotate(0)
-    for j in range(2):
+    for j in range(4):
         send(("bp", 1, j), Qs.at[zi(4), j, ha], Bp.at[0, j, ha], zn(1))
         send(("bm", 1, j), Qs.at[zi(4), j, hb], Bm.at[0, j, hb], zn(7))
     lshare(1)
@@ -323,7 +323,7 @@
     send("bpe", Qs.at[zi(3), :, hb], Bp.at[1, :, hb], zn(1))
     send("bme", Qs.at[zi(5), :, ha], Bm.at[1, :, ha], zn(7))
 
-    for j in range(2):
+    for j in range(4):
         k = zi(3)
         recv(("bp", 1, j), Bp.at[0, j, ha])
         Qs[k, j, ha] = (Qf[k, j, ha] + Bp[0, j, ha].astype(F32)).astype(BF16)
@@ -338,7 +338,7 @@
     recv("bpe", Bp.at[1, :, hb])
     recv("bme", Bm.at[1, :, ha])
     for s in (3, 4):
-        for j in range(2):
+        for j in range(4):
             k = zi(5 - s)
             recv(("bp", s - 1, j), Bp.at[s - 2, j] if s > 3 else Bp.at[1, j, ha])
             Qs[k, j] = (Qf[k, j] + Bp[s - 2, j].astype(F32)).astype(BF16)
@@ -354,20 +354,18 @@
     own[1].wait()
     own[2].wait()
     begin()
-    for j in range(2):
+    for j in range(4):
         recv(("bp", 4, j), Bp.at[3, j])
         recv(("bm", 4, j), Bm.at[3, j])
-        rows = slice(j * 256, (j + 1) * 256)
+        rows = slice(j * 128, (j + 1) * 128)
         rotated = (Qf[z, j] + Bp[3, j].astype(F32) + Bm[3, j].astype(F32)).T
         first = beta_one * mb[rows] + (1.0 - beta_one) * rotated
         second = beta_two * vb[rows] + (1.0 - beta_two) * rotated * rotated
         one = first * (1.0 / (1.0 - beta_one**STEP))
         two = second * (1.0 / (1.0 - beta_two**STEP))
-        scaled = (one / (jnp.sqrt(two) + epsilon)).astype(BF16)
-        for i in (2 * j, 2 * j + 1):
-            Sb[z, i] = scaled[(i - 2 * j) * 128:(i - 2 * j + 1) * 128]
-            same(("cp", 1, i), Sb.at[z, i], zn(1))
-            same(("cm", 1, i), Sb.at[z, i], zn(7))
+        Sb[z, j] = (one / (jnp.sqrt(two) + epsilon)).astype(BF16)
+        same(("cp", 1, j), Sb.at[z, j], zn(1))
+        same(("cm", 1, j), Sb.at[z, j], zn(7))
         fb[rows] = first
         sb[rows] = second
     outs = [pltpu.make_async_copy(fb, fo, lsem.at[3]), pltpu.make_async_copy(sb, so, lsem.at[4])]
@@ -382,15 +380,17 @@
         for d in ds:
             recv(("ss", d), So.at[zi(d)])
 
-    def back(j, first_part):
+    def back(j):
         k = (zh + rels[j]) % 4
         s = jnp.concatenate(
             [ref[2 * k + i].reshape(512, 128) for ref in (Sb, So) for i in range(2)], axis=1)
         part = jnp.dot(left(j), s, preferred_element_type=F32)
-        if first_part:
+        if j == 3:
             Ba[...] = part
+        elif j > 0:
+            Ba[...] += part
         else:
-            Ba[...] += part
+            Bk[...] = (Ba[...] + part).astype(BF16)
 
     across(0)
     for s in (2, 3):
@@ -402,27 +402,27 @@
         across(9 - s)
         across(s - 1)
     crossed(0, 1, 7)
-    back(3, True)
+    back(3)
     for j in range(2):
         recv(("cp", 3, j), Sb.at[zi(5), j])
         same(("cp", 4, j), Sb.at[zi(5), j], zn(1))
         recv(("cm", 3, j + 2), Sb.at[zi(3), j + 2])
         same(("cm", 4, j + 2), Sb.at[zi(3), j + 2], zn(7))
+    crossed(2, 6)
+    back(2)
     for j in range(2):
         recv(("cp", 3, j + 2), Sb.at[zi(5), j + 2])
         recv(("cm", 3, j), Sb.at[zi(3), j])
     across(5)
     across(3)
-    crossed(2, 6, 3, 5)
-    back(1, False)
-    back(2, False)
+    crossed(3, 5)
+    back(1)
     for j in range(2):
         recv(("cp", 4, j), Sb.at[zi(4), j])
         recv(("cm", 4, j + 2), Sb.at[zi(4), j + 2])
     across(4)
     crossed(4)
-    back(0, False)
-    Bk[...] = Ba[...].astype(BF16)
+    back(0)
     recv("rs0", Rs.at[zl])
     recv("rs1", Rs.at[1 - zl])
     def partial(k, pair_of_parts, is_own):
@@ -511,6 +511,18 @@
     assert len(slots) <= SLOTS, len(slots)
 
 
+def hand_over(a, b, c, a_out, b_out, c_out, buf, sem):
+    there = [pltpu.make_async_copy(src, buf.at[i], sem.at[i]) for i, src in enumerate((a, b, c))]
+    back = [pltpu.make_async_copy(buf.at[i], dst, sem.at[3 + i]) for i, dst in enumerate((a_out, b_out, c_out))]
+    for copy in there:
+        copy.start()
+    for i in range(3):
+        there[i].wait()
+        back[i].start()
+    for copy in back:
+        copy.wait()
+
+
 def body(gradient, first_moment, second_moment, left_basis, right_basis):
     hbm = pl.BlockSpec(memory_space=pl.ANY)
     vm = pltpu.VMEM
@@ -530,10 +542,10 @@
             vm((2, 8, 2, 128, 128), BF16),
             vm((2, 8, 128, 128), BF16),
             vm((256, 1024), BF16),
-            vm((8, 2, 128, 256), F32),
-            vm((8, 2, 128, 256), BF16),
-            vm((4, 2, 128, 256), BF16),
-            vm((4, 2, 128, 256), BF16),
+            vm((8, 4, 128, 128), F32),
+            vm((8, 4, 128, 128), BF16),
+            vm((4, 4, 128, 128), BF16),
+            vm((4, 4, 128, 128), BF16),
             vm((8, 4, 128, 128), BF16),
             vm((8, 4, 128, 128), BF16),
             vm((1024, 512), F32),
@@ -564,7 +576,15 @@
         first_moment,
         second_moment,
     )
-    return update, first_new, second_new
+    whole = jax.ShapeDtypeStruct((512, 128), F32)
+    return pl.pallas_call(
+        hand_over,
+        out_shape=(whole, whole, whole),
+        in_specs=[hbm] * 3,
+        out_specs=(hbm, hbm, hbm),
+        scratch_shapes=[vm((3, 512, 128), F32), pltpu.SemaphoreType.DMA((6,))],
+        compiler_params=pltpu.CompilerParams(vmem_limit_bytes=63 * 2**20),
+    )(update, first_new, second_new)
 
 
 def solution(mesh):

time: 108 us -> 107 us (level)
  local copies, waits for them, and re-layouts: 3.46 us -> 0 us
  Pallas kernels: 103 us -> 106 us
    unnamed x7 -> x0, local copies, waits for them, and re-layouts: 3.46 us -> none
    pallas_call x0 -> x1, Pallas kernels: none -> 1.88 us  [body(): pl.pallas_call(hand_over, out_shape=(whole, whole, whole), in_specs=[hbm]...]
where the time goes in v4:
time: 107 us
  Pallas kernels  106 us (99%)
    pallas_call x1, Pallas kernels, body(): pl.pallas_call(kernel, out_shape=(jax.ShapeDtypeStruct((512, 128), F32),...  104 us

profile of v4, /device:TPU:38, one launch (start us, length us, event | category | flops | bytes accessed | tf_op | source)
XLA Modules:
  0.0 106.6 jit_solution(6819222873089744453)
XLA Ops:
  0.6 104.1 %shard_map.76 = (f32[512,128]{1,0:T(8,128)}, f32[512,128]{1,0:T(8,128)}, f32[512,128]{1,0:T(8,128)}) custom-call(bf16[2,256,128]{2,1,0:T(8,128)(2,1)} %bitcast.3, bf16[32,512]{1,0:T(8,128)(2,1)} %l.1, bf16[8,2,128,128]{3,2,1,0:T(8,128)(2,1)} %bitcast.2, f32[512,128]{1,0:T(8,128)} %m.1, f32[512,128]{1,0:T(8,128)} %v.1), custom_call_target="tpu_custom_call" | custom-call | flops 5000000000 | bytes 10000000 | tf_op jit(solution)/shard_map/pallas_call | solution.py:529
  104.7 1.9 %shard_map.77 = (f32[512,128]{1,0:T(8,128)}, f32[512,128]{1,0:T(8,128)}, f32[512,128]{1,0:T(8,128)}) custom-call(f32[512,128]{1,0:T(8,128)} %get-tuple-element.6.a, f32[512,128]{1,0:T(8,128)} %get-tuple-element.7.b, f32[512,128]{1,0:T(8,128)} %get-tuple-element.8.c), custom_call_target="tpu_custom_call" | custom-call | tf_op jit(solution)/shard_map/pallas_call | solution.py:580

commit v5 on v4

--- a/solution.py
+++ b/solution.py
@@ -372,7 +372,6 @@
     for copy in outs:
         copy.start()
 
-    left_device(0)
     def across(d):
         send(("ss", d), Sb.at[zi(d)], So.at[zi(d)], sib)
 
@@ -448,9 +447,11 @@
                     Vb[k, j, 1, u] = low[:, at].astype(BF16)
             W[0, u, k] = kept
 
-    def send_far(u):
+    def send_far_x(u):
         send(("dx", 1, u), Vb.at[s2, lo, 1, u], Ra.at[1, u, 0], xn(1))
         send(("dx", 3, u), Vb.at[s2, hi, 1, u], Ra.at[1, u, 1], xn(3))
+
+    def send_far_y(u):
         send(("dy", 1, u), Vb.at[lo, y2, 0, u], Ra.at[0, u, 0], yn(1))
         send(("dy", 3, u), Vb.at[hi, y2, 0, u], Ra.at[0, u, 1], yn(3))
 
@@ -481,14 +482,16 @@
 
     begin()
     for i in range(2):
-        for k in (s2, sp, sm):
-            partial(k, i, False)
+        partial(s2, i, False)
+        send_far_x(2 * i)
+        send_far_x(2 * i + 1)
+        partial(sp, i, False)
+        partial(sm, i, False)
         partial(s0, i, True)
-        send_far(2 * i)
-        send_far(2 * i + 1)
+        send_far_y(2 * i)
+        send_far_y(2 * i + 1)
     send_near(0)
     send_near(1)
-    left_device(1)
     send_small(0)
     send_near(2)
     send_small(1)
@@ -504,7 +507,8 @@
         for h in range(2):
             move(h).wait_send()
 
-    left_device(2)
+    for phase in range(3):
+        left_device(phase)
     recv("f", upd)
     for copy in outs:
         copy.wait()

time: 107 us -> 106 us (level)
  no operation moved by 1% of the time
where the time goes in v5:
time: 106 us
  Pallas kernels  105 us (99%)
    pallas_call x1, Pallas kernels, body(): pl.pallas_call(kernel, out_shape=(jax.ShapeDtypeStruct((512, 128), F32),...  103 us

profile of v5, /device:TPU:38, one launch (start us, length us, event | category | flops | bytes accessed | tf_op | source)
XLA Modules:
  0.0 106.0 jit_solution(15007918530463382425)
XLA Ops:
  0.6 103.4 %shard_map.76 = (f32[512,128]{1,0:T(8,128)}, f32[512,128]{1,0:T(8,128)}, f32[512,128]{1,0:T(8,128)}) custom-call(bf16[2,256,128]{2,1,0:T(8,128)(2,1)} %bitcast.3, bf16[32,512]{1,0:T(8,128)(2,1)} %l.1, bf16[8,2,128,128]{3,2,1,0:T(8,128)(2,1)} %bitcast.2, f32[512,128]{1,0:T(8,128)} %m.1, f32[512,128]{1,0:T(8,128)} %v.1), custom_call_target="tpu_custom_call" | custom-call | flops 5000000000 | bytes 10000000 | tf_op jit(solution)/shard_map/pallas_call | solution.py:533
  104.1 1.9 %shard_map.77 = (f32[512,128]{1,0:T(8,128)}, f32[512,128]{1,0:T(8,128)}, f32[512,128]{1,0:T(8,128)}) custom-call(f32[512,128]{1,0:T(8,128)} %get-tuple-element.6.a, f32[512,128]{1,0:T(8,128)} %get-tuple-element.7.b, f32[512,128]{1,0:T(8,128)} %get-tuple-element.8.c), custom_call_target="tpu_custom_call" | custom-call | tf_op jit(solution)/shard_map/pallas_call | solution.py:584
